TPU v7x, 256 devices: a whole 4x4x8 slice. The times are simulated.
256 devices in a mesh: trade: 8 (over x, y_lo), path: 32 (over y_hi, z, core).
Axes of the slice: x: 4, y: 4 (y_hi: 2, y_lo: 2; y = y_hi * 2 + y_lo), z: 8, core: 2. Of those that a mesh axis runs over, the one named last changes fastest.
Arguments:
- coef: float32 [4, 16, 32768], P(None, None, 'trade'), may hold values from -1.5 to 1.5
- set_ids: int32 [32768], P('trade'), may hold values from 0 to 63
- bucket_ids: int32 [32768], P('trade'), may hold values from 0 to 599
- states: int32 [4, 64], P(None, 'path'), may hold values from 0 to 127
- table: float32 [4, 16, 128], replicated, may hold values from -6 to 6
- risk_weight: float32 [600], replicated, may hold values from 1 to 10
- correlation: float32 [600, 600], replicated, may hold values from 0 to 1, as said below
- date_weight: float32 [4], replicated, may hold values from 0.5 to 1.5
Outputs:
- coef_grad: float32 [4, 16, 32768], P(None, None, ('trade', 'path'))
Inputs may be any that keep to these rules, and one draw needn't show every extreme that they name: `correlation`: symmetric and positive definite with unit diagonal.
All inputs are finite; a program needn't handle non-finite values.
Results may differ from a plain program's by a relative error of at most 0.0022.
Values may be sent and summed in bfloat16 or wider, within the bound.
A program may use at most 64 MiB of HBM per device.

v0:
```python
import jax
import jax.numpy as jnp
from jax import lax
from jax.sharding import PartitionSpec as P

DATES = 4
SET_DEV = 8


def per_device(coef, set_ids, bucket_ids, states, table, risk_weight, correlation, date_weight):
    trades = coef.shape[2]
    paths = states.shape[1]
    buckets = correlation.shape[0]
    nstates = table.shape[2]
    bucket_hot = (bucket_ids[:, None] == jnp.arange(buckets)[None, :]).astype(jnp.bfloat16)
    state_hot = (states[:, :, None] == jnp.arange(nstates)[None, None, :]).astype(jnp.float32)
    bases = jnp.einsum("dps,dks->dpk", state_hot, table, precision=lax.Precision.HIGHEST)
    share = trades // lax.axis_size("path")
    out_dates = []
    for date in range(DATES):
        basis = bases[date]
        sens = jnp.dot(basis, coef[date], precision=lax.Precision.HIGHEST).astype(jnp.bfloat16)
        sens_rows = sens.T

        def margin_grad(netted, weight_now=date_weight[date]):
            weighted = netted * risk_weight
            corr_weighted = jnp.dot(
                weighted.reshape(-1, buckets), correlation, precision=lax.Precision.HIGHEST
            ).reshape(netted.shape)
            margin = jnp.sqrt(jnp.sum(weighted * corr_weighted, axis=-1) + 1.0)
            return (weight_now * risk_weight * corr_weighted / margin[..., None]).astype(
                jnp.bfloat16
            )

        partial_select = (
            set_ids[:, None] == jnp.arange(SET_DEV * lax.axis_size("trade"))[None, :]
        ).astype(jnp.bfloat16)
        left = (partial_select[:, :, None] * sens_rows[:, None, :]).reshape(
            trades, SET_DEV * lax.axis_size("trade") * paths
        )
        partial_product = lax.dot_general(
            left, bucket_hot, (((0,), (0,)), ((), ())), preferred_element_type=jnp.float32
        )
        owned = lax.psum_scatter(
            partial_product.reshape(SET_DEV * lax.axis_size("trade"), paths, buckets),
            "trade",
            scatter_dimension=0,
            tiled=True,
        )
        piece = lax.all_gather(margin_grad(owned), "trade", axis=0, tiled=True)
        count = piece.shape[0]
        product = lax.dot_general(
            piece.reshape(count * paths, buckets),
            bucket_hot,
            (((1,), (1,)), ((), ())),
            preferred_element_type=jnp.float32,
        )
        product = product.reshape(count, paths, trades)
        select = (set_ids[None, :] == jnp.arange(count)[:, None]).astype(jnp.float32)
        picked = jnp.sum(product * select[:, None, :], axis=0)

        def coef_terms(start, count, picked_now=picked, basis_now=basis):
            return jnp.dot(picked_now.T, basis_now, precision=lax.Precision.HIGHEST)

        summed = lax.psum_scatter(
            coef_terms(jnp.int32(0), share * lax.axis_size("path")),
            "path",
            scatter_dimension=0,
            tiled=True,
        )
        out_dates.append(summed.T)
    return jnp.stack(out_dates)


def solution(mesh):
    in_specs = (P(None, None, "trade"), P("trade"), P("trade"), P(None, "path"), P(), P(), P(), P())
    out_specs = P(None, None, ("trade", "path"))
    return jax.shard_map(
        per_device, mesh=mesh, in_specs=in_specs, out_specs=out_specs, check_vma=False
    )
```

profile of v0, /device:TPU:1, one launch (start us, length us, event | category | flops | bytes accessed | tf_op | source)
XLA Modules:
  0.0 673.1 jit_solution(17642705879668936940)
XLA Ops:
  6.5 0.9 copy.19
  7.4 1.0 fusion.83
  8.4 1.2 fusion.37
  9.6 1.2 fusion.38
  10.8 1.2 fusion.39
  12.0 1.2 fusion.40
  13.2 0.8 fusion.65
  14.0 4.4 broadcast_multiply_fusion.2
  18.5 1.5 mul.220
  20.0 1.5 dot_general.103
  21.5 4.4 fusion.3
  26.0 1.5 mul.210
  27.5 1.5 dot_general.96
  29.0 4.4 fusion.7
  33.4 0.2 reduce-scatter.13.cloned.1.call-start
  33.7 1.5 mul.200
  35.2 1.5 dot_general.89
  36.7 4.4 fusion.11
  41.2 1.5 mul.188
  42.7 1.5 dot_general.82
  44.2 4.5 fusion.15
  48.8 0.7 fusion.91
  49.5 2.5 broadcast_multiply_fusion.7
  52.0 12.5 %reduce-scatter.21.cloned.1.call-done = f32[8,2,600]{2,0,1:T(8,128)} async-done(((f32[64,2,600]{2,0,1:T(8,128)}), f32[8,2,600]{2,0,1:T(8,128)}) %reduce-scatter.21.cloned.1.call-update) | async-done | bytes 38416 | tf_op jit(solution)/shard_map/reduce_scatter | solution.py:44
  64.5 1.6 fusion.41
  66.2 39.3 %reduce-scatter.17.cloned.1.call-done = f32[8,2,600]{2,0,1:T(8,128)} async-done(((f32[64,2,600]{2,0,1:T(8,128)}), f32[8,2,600]{2,0,1:T(8,128)}) %reduce-scatter.17.cloned.1.call-update) | async-done | bytes 38416 | tf_op jit(solution)/shard_map/reduce_scatter | solution.py:44
  105.4 1.7 fusion.43
  107.1 39.2 %reduce-scatter.13.cloned.1.call-done = f32[8,2,600]{2,0,1:T(8,128)} async-done(((f32[64,2,600]{2,0,1:T(8,128)}), f32[8,2,600]{2,0,1:T(8,128)}) %reduce-scatter.13.cloned.1.call-update) | async-done | bytes 38416 | tf_op jit(solution)/shard_map/reduce_scatter | solution.py:44
  146.4 1.7 fusion.45
  148.1 39.3 %reduce-scatter.9.cloned.1.call-done = f32[8,2,600]{2,0,1:T(8,128)} async-done(((f32[64,2,600]{2,0,1:T(8,128)}), f32[8,2,600]{2,0,1:T(8,128)}) %reduce-scatter.9.cloned.1.call-update) | async-done | bytes 38416 | tf_op jit(solution)/shard_map/reduce_scatter | solution.py:44
  187.4 1.8 multiply_reduce_fusion.3
  189.3 22.2 %all_gather.12 = bf16[64,2,600]{2,0,1:T(8,128)(2,1)S(1)} all-gather(bf16[8,2,600]{2,0,1:T(8,128)(2,1)S(1)} %divide_convert_fusion.3), channel_id=1, replica_groups=mesh['trade'=8,'path'=32] {'trade'}, dimensions={0}, use_global_device_ids=true | all-gather | bytes 172800 | tf_op jit(solution)/shard_map/all_gather | solution.py:50
  211.4 2.4 fusion.58
  213.8 1.1 fusion.87
  215.1 21.9 %all_gather.13 = bf16[64,2,600]{2,0,1:T(8,128)(2,1)S(1)} all-gather(bf16[8,2,600]{2,0,1:T(8,128)(2,1)S(1)} %divide_convert_fusion.2), channel_id=1, replica_groups=mesh['trade'=8,'path'=32] {'trade'}, dimensions={0}, use_global_device_ids=true | all-gather | bytes 172800 | tf_op jit(solution)/shard_map/all_gather | solution.py:50
  236.9 2.4 fusion.55
  239.3 1.1 fusion.88
  240.5 22.2 %all_gather.14 = bf16[64,2,600]{2,0,1:T(8,128)(2,1)S(1)} all-gather(bf16[8,2,600]{2,0,1:T(8,128)(2,1)S(1)} %divide_convert_fusion.1), channel_id=1, replica_groups=mesh['trade'=8,'path'=32] {'trade'}, dimensions={0}, use_global_device_ids=true | all-gather | bytes 172800 | tf_op jit(solution)/shard_map/all_gather | solution.py:50
  262.7 2.4 fusion.52
  265.2 22.1 %all_gather.15 = bf16[64,2,600]{2,0,1:T(8,128)(2,1)S(1)} all-gather(bf16[8,2,600]{2,0,1:T(8,128)(2,1)S(1)} %divide_convert_fusion), channel_id=1, replica_groups=mesh['trade'=8,'path'=32] {'trade'}, dimensions={0}, use_global_device_ids=true | all-gather | bytes 172800 | tf_op jit(solution)/shard_map/all_gather | solution.py:50
  287.3 1.1 fusion.89
  288.5 2.4 fusion.49
  290.9 1.1 fusion.90
  292.0 38.0 %reduce-scatter.11.cloned.1.call-done = f32[128,16]{0,1:T(8,128)} async-done(((f32[4096,16]{0,1:T(8,128)}), f32[128,16]{0,1:T(8,128)}) %reduce-scatter.11.cloned.1.call-update) | async-done | bytes 8208 | tf_op jit(solution)/shard_map/reduce_scatter | solution.py:65
  330.0 111.5 %reduce-scatter.15.cloned.1.call-done = f32[128,16]{0,1:T(8,128)} async-done(((f32[4096,16]{0,1:T(8,128)}), f32[128,16]{0,1:T(8,128)}) %reduce-scatter.15.cloned.1.call-update) | async-done | bytes 8208 | tf_op jit(solution)/shard_map/reduce_scatter | solution.py:65
  441.5 111.7 %reduce-scatter.19.cloned.1.call-done = f32[128,16]{0,1:T(8,128)} async-done(((f32[4096,16]{0,1:T(8,128)}), f32[128,16]{0,1:T(8,128)}) %reduce-scatter.19.cloned.1.call-update) | async-done | bytes 8208 | tf_op jit(solution)/shard_map/reduce_scatter | solution.py:65
  553.2 111.7 %reduce-scatter.23.cloned.1.call-done = f32[128,16]{0,1:T(8,128)} async-done(((f32[4096,16]{0,1:T(8,128)}), f32[128,16]{0,1:T(8,128)}) %reduce-scatter.23.cloned.1.call-update) | async-done | bytes 8208 | tf_op jit(solution)/shard_map/reduce_scatter | solution.py:65
  664.9 1.4 pad_maximum_fusion
  (40 shorter events, 0.8 us)
Async XLA Ops:
  6.5 58.0 %copy-start = (f32[600,600]{1,0:T(8,128)S(1)}, f32[600,600]{1,0:T(8,128)}, u32[]{:S(2)}) copy-start(f32[600,600]{1,0:T(8,128)} %param.14) | copy-start | bytes 4320004
  6.5 58.0 %reduce-scatter.21.cloned.1.call-start = ((), (), s32[]{:S(2)}) async-start(), calls=%async_computation.14 | async-start | bytes 368640 | tf_op jit(solution)/shard_map/reduce_scatter | solution.py:44
  20.0 1.5 copy-start.7
  26.0 79.5 %reduce-scatter.17.cloned.1.call-start = ((), (), s32[]{:S(2)}) async-start(), calls=%async_computation.12 | async-start | bytes 368640 | tf_op jit(solution)/shard_map/reduce_scatter | solution.py:44
  33.4 112.9 %reduce-scatter.13.cloned.1.call-start = ((), (), s32[]{:S(2)}) async-start(), calls=%async_computation.10 | async-start | bytes 368640 | tf_op jit(solution)/shard_map/reduce_scatter | solution.py:44
  41.1 146.2 %reduce-scatter.9.cloned.1.call-start = ((), (), s32[]{:S(2)}) async-start(), calls=%async_computation.8 | async-start | bytes 368640 | tf_op jit(solution)/shard_map/reduce_scatter | solution.py:44
  44.2 4.6 copy-start.5
  44.2 4.7 copy-start.6
  44.2 5.3 copy-start.4
  48.7 281.3 %reduce-scatter.11.cloned.1.call-start = ((), (), s32[]{:S(2)}) async-start(), calls=%async_computation.9 | async-start | bytes 270336 | tf_op jit(solution)/shard_map/reduce_scatter | solution.py:65
  66.1 121.2 %copy-start.1 = (f32[8,2,600]{2,0,1:T(8,128)S(1)}, f32[8,2,600]{2,0,1:T(8,128)}, u32[]{:S(2)}) copy-start(f32[8,2,600]{2,0,1:T(8,128)} %reduce-scatter.21.cloned.1.call-done) | copy-start | bytes 115204
  105.4 82.0 %copy-start.2 = (f32[8,2,600]{2,0,1:T(8,128)S(1)}, f32[8,2,600]{2,0,1:T(8,128)}, u32[]{:S(2)}) copy-start(f32[8,2,600]{2,0,1:T(8,128)} %reduce-scatter.17.cloned.1.call-done) | copy-start | bytes 115204
  146.4 41.0 %copy-start.3 = (f32[8,2,600]{2,0,1:T(8,128)S(1)}, f32[8,2,600]{2,0,1:T(8,128)}, u32[]{:S(2)}) copy-start(f32[8,2,600]{2,0,1:T(8,128)} %reduce-scatter.13.cloned.1.call-done) | copy-start | bytes 115204
  214.9 226.6 %reduce-scatter.15.cloned.1.call-start = ((), (), s32[]{:S(2)}) async-start(), calls=%async_computation.11 | async-start | bytes 270336 | tf_op jit(solution)/shard_map/reduce_scatter | solution.py:65
  265.1 288.1 %reduce-scatter.19.cloned.1.call-start = ((), (), s32[]{:S(2)}) async-start(), calls=%async_computation.13 | async-start | bytes 270336 | tf_op jit(solution)/shard_map/reduce_scatter | solution.py:65
  288.5 376.4 %reduce-scatter.23.cloned.1.call-start = ((), (), s32[]{:S(2)}) async-start(), calls=%async_computation.15 | async-start | bytes 270336 | tf_op jit(solution)/shard_map/reduce_scatter | solution.py:65
Sparse Core Ops, SparseCore 0:
  26.1 38.3 reduce-scatter.20
  67.2 38.2 reduce-scatter.16
  107.9 38.3 reduce-scatter.12
  148.9 38.4 reduce-scatter.8
  215.0 114.9 reduce-scatter.10
  333.7 107.7 reduce-scatter.14
  445.4 107.7 reduce-scatter.18
  557.1 107.7 reduce-scatter.22
where the time goes:
time: 679 us; the launch traced here: 673 us
  waiting for transfers between devices  503 us (74%)
  blocking collectives  88.3 us (13%)
  matrix products  44.3 us (7%)
  between operations  13.7 us (2%)
  local copies, waits for them, and re-layouts  13.5 us (2%)
  other arithmetic  9.51 us (1%)
    reduce_scatter x4, waiting for transfers between devices, per_device(): lax.psum_scatter(coef_terms(jnp.int32(0), share * lax.axis_size('path')),...  373 us
    reduce_scatter x4, waiting for transfers between devices, per_device(): lax.psum_scatter(partial_product.reshape(SET_DEV * lax.axis_size('trade')...  130 us
    all_gather x4, blocking collectives, per_device(): piece = lax.all_gather(margin_grad(owned), 'trade', axis=0, tiled=True)  88.3 us
    dot_general x4, matrix products, per_device(): lax.dot_general(left, bucket_hot, (((0,), (0,)), ((), ())), preferred_ele...  17.8 us
  transfers between devices with their start and end apart: 8, of which 8 were waited for; matrix products, arithmetic and copies ran while one was open for 6% of the time, Pallas kernels for 0%

commit v1 on v0

v1 whole, which is shorter than its diff:
```python
import functools

import jax
import jax.numpy as jnp
from jax import lax
from jax.experimental import pallas as pl
from jax.experimental.pallas import tpu as pltpu
from jax.sharding import PartitionSpec as P

DATES = 4
SETS = 64
LO = 256
GROUPS = 3
HI = GROUPS * SETS
LANES = 128
MESH = pl.DeviceIdType.MESH
BF = jnp.bfloat16
F32 = jnp.float32
NT = (((1,), (1,)), ((), ()))


def split3(x):
    a = x.astype(BF)
    r = x - a.astype(F32)
    b = r.astype(BF)
    c = (r - b.astype(F32)).astype(BF)
    return a, b, c


def kernel(
    nt,
    npath,
    coef_ref,
    set_ref,
    bkt_ref,
    st_ref,
    table_ref,
    rw_ref,
    corr_ref,
    dw_ref,
    out_ref,
    part,
    sens_out,
    sens_in,
    cell_in,
    hi_f,
    lo_f,
    s_f,
    acc,
    chi,
    clo,
    grad,
    tgp,
    tg,
    tg_in,
    tgx,
    pr,
    st_out,
    st_in,
    sens_ss,
    sens_rs,
    cell_ss,
    cell_rs,
    tg_ss,
    tg_rs,
    st_ss,
    st_rs,
    pr_ss,
    pr_rs,
):
    me = lax.axis_index("trade")
    mp = lax.axis_index("path")
    rows = set_ref.shape[0]
    nb = corr_ref.shape[0]

    barrier = pltpu.get_barrier_semaphore()
    for r in range(1, nt):
        pl.semaphore_signal(
            barrier, inc=1, device_id={"trade": lax.rem(me + r, nt)}, device_id_type=MESH
        )

    def greet(r, c):
        pl.semaphore_signal(
            barrier, inc=1, device_id={"path": lax.rem(mp + r, npath)}, device_id_type=MESH
        )
        return c

    lax.fori_loop(1, npath, greet, 0)

    bkt = bkt_ref[...]
    group = (bkt >= LO).astype(jnp.int32) + (bkt >= 2 * LO).astype(jnp.int32)
    hi = group * SETS + set_ref[...]
    lo = bkt - group * LO
    cell_in[me] = hi * LO + lo

    lane = lax.broadcasted_iota(jnp.int32, table_ref.shape[1:], 1)
    for d in range(DATES):
        for p in range(nt // DATES):
            q = d * (nt // DATES) + p
            state = st_ref[d, p]
            st_out[q : q + 1, :] = jnp.full((1, LANES), state, jnp.int32).astype(F32)
            col = jnp.sum(
                jnp.where(lane == state, table_ref[d], 0.0), axis=1, keepdims=True
            )
            for c in range(rows):
                x = coef_ref[d, :, c * LANES : (c + 1) * LANES] * col
                part[c * 8 : (c + 1) * 8, :] = x[:8] + x[8:]
            for g in range(rows // 8):
                tot = part[pl.ds(g * 64, 8, stride=8), :]
                for s in range(1, 8):
                    tot = tot + part[pl.ds(g * 64 + s, 8, stride=8), :]
                s_f[g * 8 : (g + 1) * 8, :] = tot
            sens_out[q] = s_f[0:rows, :].astype(BF)

    pl.semaphore_wait(barrier, nt - 1 + npath - 1)

    def trade_copies(r):
        peer = lax.rem(me + r, nt)
        return (
            pltpu.make_async_remote_copy(
                src_ref=cell_in.at[me],
                dst_ref=cell_in.at[me],
                send_sem=cell_ss.at[r],
                recv_sem=cell_rs.at[r],
                device_id={"trade": peer},
                device_id_type=MESH,
            ),
            pltpu.make_async_remote_copy(
                src_ref=sens_out.at[peer],
                dst_ref=sens_in.at[me],
                send_sem=sens_ss.at[r],
                recv_sem=sens_rs.at[r],
                device_id={"trade": peer},
                device_id_type=MESH,
            ),
        )

    for r in range(1, nt):
        for copy in trade_copies(r):
            copy.start()
    sens_in[me] = sens_out[me]

    def send_state(r, c):
        pltpu.make_async_remote_copy(
            src_ref=st_out,
            dst_ref=st_in.at[mp],
            send_sem=st_ss,
            recv_sem=st_rs,
            device_id={"path": lax.rem(mp + r, npath)},
            device_id_type=MESH,
        ).start()
        return c

    lax.fori_loop(1, npath, send_state, 0)
    st_in[mp] = st_out[...]

    chi[...] = jnp.zeros_like(chi)
    clo[...] = jnp.zeros_like(clo)
    corr = corr_ref[...]
    top = corr.astype(BF)
    chi[0:nb, 0:nb] = top
    clo[0:nb, 0:nb] = (corr - top.astype(F32)).astype(BF)

    acc[...] = jnp.zeros_like(acc)
    hi_iota = lax.broadcasted_iota(jnp.int32, (HI, LANES), 0).astype(F32).astype(BF)
    lo_iota = lax.broadcasted_iota(jnp.int32, (LO, LANES), 0).astype(F32).astype(BF)
    one, zero = jnp.ones((), BF), jnp.zeros((), BF)

    def spread(ref, row, n):
        x = jnp.broadcast_to(ref[pl.ds(row, 1), :], (16, LANES)).astype(BF)
        return jnp.broadcast_to(x[None], (n // 16, 16, LANES)).reshape(n, LANES)

    def bucket_hot(row):
        return jnp.where(spread(lo_f, row, LO) == lo_iota, one, zero)

    def set_hot(row):
        return jnp.where(spread(hi_f, row, HI) == hi_iota, spread(s_f, row, HI), zero)

    def net_block(src):
        base = pl.multiple_of(src * rows, rows)
        cells = cell_in[src]
        h = lax.shift_right_logical(cells, 8)
        hi_f[pl.ds(base, rows), :] = h.astype(F32)
        lo_f[pl.ds(base, rows), :] = (cells - h * LO).astype(F32)
        s_f[pl.ds(base, rows), :] = sens_in[src].astype(F32)

        def step(g, c):
            row = base + g * 8
            left = jnp.concatenate([set_hot(row + i) for i in range(8)], axis=1)
            right = jnp.concatenate([bucket_hot(row + i) for i in range(8)], axis=1)
            acc[...] += lax.dot_general(left, right, NT, preferred_element_type=F32)
            return c

        lax.fori_loop(0, rows // 8, step, 0)

    net_block(me)

    def net_from(r, c):
        for copy in trade_copies(r):
            copy.wait_recv()
        net_block(lax.rem(me + nt - r, nt))
        return c

    lax.fori_loop(1, nt, net_from, 0)

    rw = rw_ref[...]
    weighted = [acc[g * SETS : (g + 1) * SETS, :] * rw[:, g * LO : (g + 1) * LO] for g in range(GROUPS)]
    w = jnp.concatenate(weighted, axis=1)
    w_hi = w.astype(BF)
    w_lo = (w - w_hi.astype(F32)).astype(BF)
    cw = (
        jnp.dot(w_hi, chi[...], preferred_element_type=F32)
        + jnp.dot(w_hi, clo[...], preferred_element_type=F32)
        + jnp.dot(w_lo, chi[...], preferred_element_type=F32)
    )
    margin = jnp.sqrt(jnp.sum(w * cw, axis=1, keepdims=True) + 1.0)
    weight = dw_ref[me // (nt // DATES)]
    net_grad = ((weight * rw) * cw / margin).astype(BF)
    for g in range(GROUPS):
        grad[g * SETS : (g + 1) * SETS, :] = net_grad[:, g * LO : (g + 1) * LO]

    hi_iota8 = lax.broadcasted_iota(jnp.int32, (HI, LANES), 0).astype(F32)

    def pick_block(dst):
        base = pl.multiple_of(dst * rows, rows)

        def step(g, c):
            row = pl.multiple_of(base + g * 8, 8)
            right = jnp.concatenate([bucket_hot(row + i) for i in range(8)], axis=1)
            product = jnp.dot(grad[...], right, preferred_element_type=F32)
            for i in range(8):
                h = jnp.broadcast_to(hi_f[pl.ds(row + i, 1), :], (HI, LANES))
                kept = jnp.where(h == hi_iota8, product[:, i * LANES : (i + 1) * LANES], 0.0)
                tgp[i * 8 : (i + 1) * 8, :] = jnp.sum(kept.reshape(HI // 8, 8, LANES), axis=0)
            tot = tgp[pl.ds(0, 8, stride=8), :]
            for s in range(1, 8):
                tot = tot + tgp[pl.ds(s, 8, stride=8), :]
            tg[pl.ds(row, 8), :] = tot
            return c

        lax.fori_loop(0, rows // 8, step, 0)

    def pick_copy(r):
        peer = lax.rem(me + r, nt)
        return pltpu.make_async_remote_copy(
            src_ref=tg.at[pl.ds(pl.multiple_of(peer * rows, rows), rows)],
            dst_ref=tg_in.at[pl.ds(pl.multiple_of(me * rows, rows), rows)],
            send_sem=tg_ss.at[r],
            recv_sem=tg_rs.at[r],
            device_id={"trade": peer},
            device_id_type=MESH,
        )

    def pick_to(r, c):
        pick_block(lax.rem(me + r, nt))
        pick_copy(r).start()
        return c

    lax.fori_loop(1, nt, pick_to, 0)
    pick_block(me)
    own = pl.ds(pl.multiple_of(me * rows, rows), rows)
    tg_in[own, :] = tg[own, :]
    for r in range(1, nt):
        pick_copy(r).wait_recv()

    for c in range(rows):
        tgx[c] = tg_in[pl.ds(c, nt, stride=rows), :]

    def send_grad(r, c):
        peer = lax.rem(mp + r, npath)
        pltpu.make_async_remote_copy(
            src_ref=tgx.at[peer],
            dst_ref=pr.at[mp],
            send_sem=pr_ss,
            recv_sem=pr_rs,
            device_id={"path": peer},
            device_id_type=MESH,
        ).start()
        return c

    lax.fori_loop(1, npath, send_grad, 0)
    pr[mp] = tgx[mp]

    others = pl.ds(0, npath - 1)
    pltpu.make_async_copy(st_in.at[others], st_in.at[others], st_rs).wait()
    pairs = npath * nt
    ks = table_ref.shape[1]
    states = st_in[...].reshape(pairs, LANES)
    hot = (states == lax.broadcasted_iota(jnp.int32, (pairs, LANES), 1).astype(F32)).astype(F32).astype(BF)
    tab = table_ref[...].reshape(DATES * ks, LANES)
    at_date = lax.broadcasted_iota(jnp.int32, (DATES * ks, pairs), 0) // ks
    pair_date = (lax.broadcasted_iota(jnp.int32, (DATES * ks, pairs), 1) % nt) // (nt // DATES)
    basis = [
        jnp.where(
            at_date == pair_date, lax.dot_general(t, hot, NT, preferred_element_type=F32), 0.0
        ).astype(BF)
        for t in split3(tab)
    ]

    pltpu.make_async_copy(pr.at[others], pr.at[others], pr_rs).wait()
    right = pr[...].reshape(pairs, LANES).astype(BF)
    total = jnp.dot(basis[0], right, preferred_element_type=F32)
    for b in basis[1:]:
        total = total + jnp.dot(b, right, preferred_element_type=F32)
    out_ref[...] = total.reshape(DATES, ks, LANES)

    for r in range(1, nt):
        for copy in trade_copies(r):
            copy.wait_send()
        pick_copy(r).wait_send()
    pltpu.make_async_copy(st_in.at[others], st_in.at[others], st_ss).wait()
    pltpu.make_async_copy(pr.at[others], pr.at[others], pr_ss).wait()


def per_device(coef, set_ids, bucket_ids, states, table, risk_weight, correlation, date_weight):
    nt = lax.axis_size("trade")
    npath = lax.axis_size("path")
    trades = coef.shape[2]
    rows = trades // LANES
    nb = correlation.shape[0]
    ks = table.shape[1]
    vmem = pl.BlockSpec(memory_space=pltpu.VMEM)
    smem = pl.BlockSpec(memory_space=pltpu.SMEM)
    rw = jnp.pad(risk_weight, (0, GROUPS * LO - nb)).reshape(1, GROUPS * LO)
    dma = pltpu.SemaphoreType.DMA
    return pl.pallas_call(
        functools.partial(kernel, nt, npath),
        out_shape=jax.ShapeDtypeStruct((DATES, ks, LANES), F32),
        in_specs=[vmem, vmem, vmem, smem, vmem, vmem, vmem, smem],
        out_specs=vmem,
        scratch_shapes=[
            pltpu.VMEM((rows * 8, LANES), F32),
            pltpu.VMEM((nt, rows, LANES), BF),
            pltpu.VMEM((nt, rows, LANES), BF),
            pltpu.VMEM((nt, rows, LANES), jnp.int32),
            pltpu.VMEM((nt * rows, LANES), F32),
            pltpu.VMEM((nt * rows, LANES), F32),
            pltpu.VMEM((nt * rows, LANES), F32),
            pltpu.VMEM((HI, LO), F32),
            pltpu.VMEM((GROUPS * LO, GROUPS * LO), BF),
            pltpu.VMEM((GROUPS * LO, GROUPS * LO), BF),
            pltpu.VMEM((HI, LO), BF),
            pltpu.VMEM((64, LANES), F32),
            pltpu.VMEM((nt * rows, LANES), F32),
            pltpu.VMEM((nt * rows, LANES), F32),
            pltpu.VMEM((npath, nt, LANES), F32),
            pltpu.VMEM((npath, nt, LANES), F32),
            pltpu.VMEM((nt, LANES), F32),
            pltpu.VMEM((npath, nt, LANES), F32),
            dma((nt,)),
            dma((nt,)),
            dma((nt,)),
            dma((nt,)),
            dma((nt,)),
            dma((nt,)),
            dma,
            dma,
            dma,
            dma,
        ],
        compiler_params=pltpu.CompilerParams(
            collective_id=0, has_side_effects=True, vmem_limit_bytes=48 * 1024 * 1024
        ),
    )(
        coef,
        set_ids.reshape(rows, LANES),
        bucket_ids.reshape(rows, LANES),
        states,
        table,
        rw,
        correlation,
        date_weight,
    )


def solution(mesh):
    in_specs = (P(None, None, "trade"), P("trade"), P("trade"), P(None, "path"), P(), P(), P(), P())
    out_specs = P(None, None, ("trade", "path"))
    return jax.shard_map(
        per_device, mesh=mesh, in_specs=in_specs, out_specs=out_specs, check_vma=False
    )
```

time: 679 us -> 50.4 us (0.07)
  waiting for transfers between devices: 503 us -> 0 us
  blocking collectives: 88.3 us -> 0 us
  matrix products: 44.3 us -> 0 us
  Pallas kernels: 0 us -> 42.2 us
  between operations: 13.7 us -> 0.02 us
  other arithmetic: 9.51 us -> 0 us
    reduce_scatter x8 -> x0, waiting for transfers between devices: 503 us -> none  [the longest x4 373 us: per_device(): lax.psum_scatter(coef_terms(jnp.int32(0), share * lax.axis_size('path')),...]
    all_gather x4 -> x0, blocking collectives: 88.3 us -> none  [per_device(): piece = lax.all_gather(margin_grad(owned), 'trade', axis=0, tiled=True)]
    dot_general x21 -> x0, matrix products: 44.3 us -> none  [the longest x4 17.8 us: per_device(): lax.dot_general(left, bucket_hot, (((0,), (0,)), ((), ())), preferred_ele...]
    pallas_call x0 -> x1, Pallas kernels: none -> 42.2 us  [per_device(): pl.pallas_call(functools.partial(kernel, nt, npath), out_shape=jax.ShapeD...]
    mul x2 -> x0, other arithmetic: 6.9 us -> none  [the longest x1 4.45 us: per_device(): partial_select[:, :, None] * sens_rows[:, None, :]]
  transfers between devices with their start and end apart: 8 -> 0, of which waited for: 8 -> 0; matrix products, arithmetic and copies ran while one was open for 6% -> 0% of each run, Pallas kernels for 0% -> 0%
where the time goes in v1:
time: 50.4 us; the launch traced here: 49.7 us
  Pallas kernels  42.2 us (84%)
  local copies, waits for them, and re-layouts  7.54 us (15%)
    pallas_call x1, Pallas kernels, per_device(): pl.pallas_call(functools.partial(kernel, nt, npath), out_shape=jax.ShapeD...  42.2 us
    unnamed x14, local copies, waits for them, and re-layouts  6.85 us

profile of v1, /device:TPU:1, one launch (start us, length us, event | category | flops | bytes accessed | tf_op | source)
XLA Modules:
  0.0 49.7 jit_solution(10709397465566169902)
XLA Ops:
  0.0 0.8 %copy.9.st_ref = s32[4,2]{1,0:T(4,128)S(1)} copy(s32[4,2]{0,1:T(2,128)} %param.11) | data formatting | bytes 64 | tf_op args[3]
  0.8 0.7 %pad.4 = f32[768]{0:T(1024)S(1)} pad(f32[600]{0:T(1024)} %param.13, f32[]{:T(128)} %constant.2.clone.1), padding=0_168 | pad | bytes 5476 | tf_op jit(solution)/shard_map/jit(_pad)/pad | solution.py:324
  1.5 0.0 copy-start
  1.5 1.4 %copy-done = f32[600,600]{1,0:T(8,128)S(1)} copy-done((f32[600,600]{1,0:T(8,128)S(1)}, f32[600,600]{1,0:T(8,128)}, u32[]{:S(2)}) %copy-start) | copy-done | bytes 1440024
  2.9 0.0 copy-start.1
  2.9 1.2 %copy-done.1 = f32[4,16,4096]{2,1,0:T(8,128)S(1)} copy-done((f32[4,16,4096]{2,1,0:T(8,128)S(1)}, f32[4,16,4096]{2,1,0:T(8,128)}, u32[]{:S(2)}) %copy-start.1) | copy-done | bytes 1048600
  4.1 0.0 copy-start.2
  4.1 0.8 %copy-done.2 = f32[4,16,128]{2,1,0:T(8,128)S(1)} copy-done((f32[4,16,128]{2,1,0:T(8,128)S(1)}, f32[4,16,128]{2,1,0:T(8,128)}, u32[]{:S(2)}) %copy-start.2) | copy-done | bytes 32792
  4.8 0.0 copy-start.3
  4.8 0.7 %copy-done.3 = s32[4096]{0:T(1024)S(1)} copy-done((s32[4096]{0:T(1024)S(1)}, s32[4096]{0:T(1024)}, u32[]{:S(2)}) %copy-start.3) | copy-done | bytes 16408
  5.6 0.0 copy-start.4
  5.6 0.7 %copy-done.4 = s32[4096]{0:T(1024)S(1)} copy-done((s32[4096]{0:T(1024)S(1)}, s32[4096]{0:T(1024)}, u32[]{:S(2)}) %copy-start.4) | copy-done | bytes 16408
  6.3 0.0 copy-start.5
  6.3 0.7 %copy-done.5 = f32[4]{0:T(128)S(1)} copy-done((f32[4]{0:T(128)S(1)}, f32[4]{0:T(128)}, u32[]{:S(2)}) %copy-start.5) | copy-done | bytes 40
  6.9 42.2 %shard_map.82 = f32[4,16,128]{2,1,0:T(8,128)S(1)} custom-call(f32[4,16,4096]{2,1,0:T(8,128)S(1)} %copy-done.1, s32[32,128]{1,0:T(8,128)S(1)} %bitcast.2, s32[32,128]{1,0:T(8,128)S(1)} %bitcast.3, s32[4,2]{1,0:T(4,128)S(1)} %copy.9.st_ref, f32[4,16,128]{2,1,0:T(8,128)S(1)} %copy-done.2, f32[1,768]{1,0:T(1,128)S(1)} %reshape.11.rw_ref, ...), custom_call_target="tpu_custom_call" | custom-call | tf_op jit(solution)/shard_map/pallas_call | solution.py:326
  49.1 0.6 %copy.11 = f32[4,16,128]{2,1,0:T(8,128)} copy(f32[4,16,128]{2,1,0:T(8,128)S(1)} %shard_map.82) | data formatting | bytes 65536
  (1 shorter events, 0.0 us)
Async XLA Ops:
  1.5 1.4 %copy-start = (f32[600,600]{1,0:T(8,128)S(1)}, f32[600,600]{1,0:T(8,128)}, u32[]{:S(2)}) copy-start(f32[600,600]{1,0:T(8,128)} %corr_ref.1) | copy-start | bytes 4320004
  2.9 1.2 %copy-start.1 = (f32[4,16,4096]{2,1,0:T(8,128)S(1)}, f32[4,16,4096]{2,1,0:T(8,128)}, u32[]{:S(2)}) copy-start(f32[4,16,4096]{2,1,0:T(8,128)} %coef_ref.1) | copy-start | bytes 3145732
  4.1 0.8 %copy-start.2 = (f32[4,16,128]{2,1,0:T(8,128)S(1)}, f32[4,16,128]{2,1,0:T(8,128)}, u32[]{:S(2)}) copy-start(f32[4,16,128]{2,1,0:T(8,128)} %table_ref.1) | copy-start | bytes 98308
  4.8 0.7 %copy-start.3 = (s32[4096]{0:T(1024)S(1)}, s32[4096]{0:T(1024)}, u32[]{:S(2)}) copy-start(s32[4096]{0:T(1024)} %param.9) | copy-start | bytes 49156
  5.6 0.7 %copy-start.4 = (s32[4096]{0:T(1024)S(1)}, s32[4096]{0:T(1024)}, u32[]{:S(2)}) copy-start(s32[4096]{0:T(1024)} %param.10) | copy-start | bytes 49156
  6.3 0.7 %copy-start.5 = (f32[4]{0:T(128)S(1)}, f32[4]{0:T(128)}, u32[]{:S(2)}) copy-start(f32[4]{0:T(128)} %dw_ref.1) | copy-start | bytes 52

commit v2 on v1

--- a/solution.py
+++ b/solution.py
@@ -30,6 +30,15 @@
 def kernel(
     nt,
     npath,
+    coef_hbm,
+    set_hbm,
+    bkt_hbm,
+    st_hbm,
+    table_hbm,
+    rw_hbm,
+    corr_hbm,
+    dw_hbm,
+    out_ref,
     coef_ref,
     set_ref,
     bkt_ref,
@@ -38,7 +47,7 @@
     rw_ref,
     corr_ref,
     dw_ref,
-    out_ref,
+    load_sem,
     part,
     sens_out,
     sens_in,
@@ -73,6 +82,24 @@
     rows = set_ref.shape[0]
     nb = corr_ref.shape[0]
 
+    loads = [
+        pltpu.make_async_copy(src, dst, load_sem.at[i])
+        for i, (src, dst) in enumerate(
+            (
+                (set_hbm, set_ref),
+                (bkt_hbm, bkt_ref),
+                (st_hbm, st_ref),
+                (table_hbm, table_ref),
+                (coef_hbm, coef_ref),
+                (corr_hbm, corr_ref),
+                (rw_hbm, rw_ref),
+                (dw_hbm, dw_ref),
+            )
+        )
+    ]
+    for load in loads:
+        load.start()
+
     barrier = pltpu.get_barrier_semaphore()
     for r in range(1, nt):
         pl.semaphore_signal(
@@ -87,17 +114,21 @@
 
     lax.fori_loop(1, npath, greet, 0)
 
+    loads[0].wait()
+    loads[1].wait()
     bkt = bkt_ref[...]
     group = (bkt >= LO).astype(jnp.int32) + (bkt >= 2 * LO).astype(jnp.int32)
     hi = group * SETS + set_ref[...]
     lo = bkt - group * LO
     cell_in[me] = hi * LO + lo
 
+    for load in loads[2:5]:
+        load.wait()
     lane = lax.broadcasted_iota(jnp.int32, table_ref.shape[1:], 1)
     for d in range(DATES):
         for p in range(nt // DATES):
             q = d * (nt // DATES) + p
-            state = st_ref[d, p]
+            state = st_ref[p, d]
             st_out[q : q + 1, :] = jnp.full((1, LANES), state, jnp.int32).astype(F32)
             col = jnp.sum(
                 jnp.where(lane == state, table_ref[d], 0.0), axis=1, keepdims=True
@@ -154,6 +185,7 @@
     lax.fori_loop(1, npath, send_state, 0)
     st_in[mp] = st_out[...]
 
+    loads[5].wait()
     chi[...] = jnp.zeros_like(chi)
     clo[...] = jnp.zeros_like(clo)
     corr = corr_ref[...]
@@ -203,7 +235,9 @@
 
     lax.fori_loop(1, nt, net_from, 0)
 
-    rw = rw_ref[...]
+    loads[6].wait()
+    loads[7].wait()
+    rw = jnp.concatenate([rw_ref[...].reshape(1, nb), jnp.zeros((1, GROUPS * LO - nb), F32)], axis=1)
     weighted = [acc[g * SETS : (g + 1) * SETS, :] * rw[:, g * LO : (g + 1) * LO] for g in range(GROUPS)]
     w = jnp.concatenate(weighted, axis=1)
     w_hi = w.astype(BF)
@@ -320,15 +354,23 @@
     nb = correlation.shape[0]
     ks = table.shape[1]
     vmem = pl.BlockSpec(memory_space=pltpu.VMEM)
-    smem = pl.BlockSpec(memory_space=pltpu.SMEM)
-    rw = jnp.pad(risk_weight, (0, GROUPS * LO - nb)).reshape(1, GROUPS * LO)
+    hbm = pl.BlockSpec(memory_space=pltpu.HBM)
     dma = pltpu.SemaphoreType.DMA
     return pl.pallas_call(
         functools.partial(kernel, nt, npath),
         out_shape=jax.ShapeDtypeStruct((DATES, ks, LANES), F32),
-        in_specs=[vmem, vmem, vmem, smem, vmem, vmem, vmem, smem],
+        in_specs=[hbm] * 8,
         out_specs=vmem,
         scratch_shapes=[
+            pltpu.VMEM(coef.shape, F32),
+            pltpu.VMEM((rows, LANES), jnp.int32),
+            pltpu.VMEM((rows, LANES), jnp.int32),
+            pltpu.SMEM(states.shape[::-1], jnp.int32),
+            pltpu.VMEM(table.shape, F32),
+            pltpu.VMEM((nb,), F32),
+            pltpu.VMEM(correlation.shape, F32),
+            pltpu.SMEM(date_weight.shape, F32),
+            dma((8,)),
             pltpu.VMEM((rows * 8, LANES), F32),
             pltpu.VMEM((nt, rows, LANES), BF),
             pltpu.VMEM((nt, rows, LANES), BF),
@@ -359,15 +401,15 @@
             dma,
         ],
         compiler_params=pltpu.CompilerParams(
-            collective_id=0, has_side_effects=True, vmem_limit_bytes=48 * 1024 * 1024
+            collective_id=0, has_side_effects=True, vmem_limit_bytes=62 * 1024 * 1024
         ),
     )(
         coef,
         set_ids.reshape(rows, LANES),
         bucket_ids.reshape(rows, LANES),
-        states,
+        states.T,
         table,
-        rw,
+        risk_weight,
         correlation,
         date_weight,
     )

time: 50.4 us -> 44.2 us (0.88)
  local copies, waits for them, and re-layouts: 7.54 us -> 1.38 us
    unnamed x14 -> x1, local copies, waits for them, and re-layouts: 6.85 us -> 1.38 us
    pad x1 -> x0, local copies, waits for them, and re-layouts: 0.69 us -> none  [per_device(): rw = jnp.pad(risk_weight, (0, GROUPS * LO - nb)).reshape(1, GROUPS * LO)]
where the time goes in v2:
time: 44.2 us; the launch traced here: 43.6 us
  Pallas kernels  42.2 us (95%)
  local copies, waits for them, and re-layouts  1.38 us (3%)
    pallas_call x1, Pallas kernels, per_device(): pl.pallas_call(functools.partial(kernel, nt, npath), out_shape=jax.ShapeD...  42.2 us
    unnamed x1, local copies, waits for them, and re-layouts  1.38 us

profile of v2, /device:TPU:1, one launch (start us, length us, event | category | flops | bytes accessed | tf_op | source)
XLA Modules:
  0.0 43.6 jit_solution(17048058931560655462)
XLA Ops:
  0.0 42.2 %shard_map.82 = f32[4,16,128]{2,1,0:T(8,128)} custom-call(f32[4,16,4096]{2,1,0:T(8,128)} %coef_hbm.1, s32[32,128]{1,0:T(8,128)} %bitcast.3, s32[32,128]{1,0:T(8,128)} %bitcast.4, s32[2,4]{1,0:T(2,128)} %bitcast.5, f32[4,16,128]{2,1,0:T(8,128)} %table_hbm.1, f32[600]{0:T(1024)} %rw_hbm.1, f32[600,600]{1,0:T(8,128)} %corr_hbm.1, f32[4]{0:T(128)} %dw_hbm.1), custom_call_target="tpu_custom_call" | custom-call | tf_op jit(solution)/shard_map/pallas_call | solution.py:359
  42.3 1.4 %copy.10 = f32[4,16,128]{2,1,0:T(8,128)} copy(f32[4,16,128]{2,1,0:T(8,128)} %shard_map.82) | data formatting | bytes 65536

commit v3 on v2

v3 whole, which is shorter than its diff:
```python
import functools

import jax
import jax.numpy as jnp
from jax import lax
from jax.experimental import pallas as pl
from jax.experimental.pallas import tpu as pltpu
from jax.sharding import PartitionSpec as P

DATES = 4
SETS = 64
LO = 256
GROUPS = 3
HI = GROUPS * SETS
LANES = 128
MESH = pl.DeviceIdType.MESH
BF = jnp.bfloat16
F32 = jnp.float32
NT = (((1,), (1,)), ((), ()))


def split3(x):
    a = x.astype(BF)
    r = x - a.astype(F32)
    b = r.astype(BF)
    c = (r - b.astype(F32)).astype(BF)
    return a, b, c


def kernel(
    nt,
    npath,
    coef_hbm,
    set_hbm,
    bkt_hbm,
    st_hbm,
    table_hbm,
    rw_hbm,
    corr_hbm,
    dw_hbm,
    out_ref,
    coef_ref,
    set_ref,
    bkt_ref,
    st_ref,
    table_ref,
    rw_ref,
    corr_ref,
    dw_ref,
    part,
    sens_out,
    sens_in,
    cell_in,
    hi_f,
    lo_f,
    s_f,
    acc,
    chi,
    clo,
    grad,
    tgp,
    tg,
    tg_in,
    tgx,
    msg,
    pr,
    st_out,
    st_in,
    load_sem,
    sens_ss,
    sens_rs,
    cell_ss,
    cell_rs,
    tg_ss,
    tg_rs,
    st_ss,
    st_rs,
    sib_ss,
    sib_rs,
    pr_ss,
    pr_rs,
):
    me = lax.axis_index("trade")
    mp = lax.axis_index("path")
    core = lax.rem(mp, 2)
    chip = mp // 2
    nchip = npath // 2
    rows = set_ref.shape[0]
    half = rows // 2
    nb = corr_ref.shape[0]
    per_date = nt // DATES

    def device(r, other):
        path = mp + other * (1 - 2 * core)
        return {"trade": lax.rem(me + r, nt), "path": path}

    def along(k):
        return {"path": lax.rem(chip + k, nchip) * 2 + core}

    loads = [
        pltpu.make_async_copy(src, dst, load_sem.at[i])
        for i, (src, dst) in enumerate(
            (
                (coef_hbm, coef_ref),
                (table_hbm, table_ref),
                (st_hbm, st_ref),
                (set_hbm, set_ref),
                (bkt_hbm, bkt_ref),
                (corr_hbm, corr_ref),
                (rw_hbm, rw_ref),
                (dw_hbm, dw_ref),
            )
        )
    ]
    for load in loads:
        load.start()

    barrier = pltpu.get_barrier_semaphore()
    for r in range(nt):
        for other in range(2):
            if r or other:
                pl.semaphore_signal(
                    barrier, inc=1, device_id=device(r, other), device_id_type=MESH
                )

    def greet(k, c):
        pl.semaphore_signal(barrier, inc=1, device_id=along(k), device_id_type=MESH)
        return c

    lax.fori_loop(1, nchip, greet, 0)

    loads[3].wait()
    loads[4].wait()
    for p in range(2):
        every = pl.ds(p, half, stride=2)
        bkt = bkt_ref[every, :]
        group = (bkt >= LO).astype(jnp.int32) + (bkt >= 2 * LO).astype(jnp.int32)
        cell_in[0, p * half : (p + 1) * half, :] = (
            (group * SETS + set_ref[every, :]) * LO + bkt - group * LO
        )

    for load in loads[:3]:
        load.wait()
    lane = lax.broadcasted_iota(jnp.int32, table_ref.shape[1:], 1)
    for d in range(DATES):
        for p in range(per_date):
            q = d * per_date + p
            state = st_ref[p, d]
            st_out[core, q : q + 1, :] = jnp.full((1, LANES), state, jnp.int32).astype(F32)
            col = jnp.sum(
                jnp.where(lane == state, table_ref[d], 0.0), axis=1, keepdims=True
            )
            for c in range(rows):
                x = coef_ref[d, :, c * LANES : (c + 1) * LANES] * col
                at = (c % 2) * half + c // 2
                part[at * 8 : (at + 1) * 8, :] = x[:8] + x[8:]
            tots = []
            for g in range(rows // 8):
                tot = part[pl.ds(g * 64, 8, stride=8), :]
                for s in range(1, 8):
                    tot = tot + part[pl.ds(g * 64 + s, 8, stride=8), :]
                tots.append(tot)
            sens_out[q] = jnp.concatenate(tots, axis=0).astype(BF)

    pl.semaphore_wait(barrier, 2 * nt - 1 + nchip - 1)

    def trade_copies(r):
        peer = lax.rem(me + r, nt)
        return (
            pltpu.make_async_remote_copy(
                src_ref=cell_in.at[0],
                dst_ref=cell_in.at[r],
                send_sem=cell_ss.at[r],
                recv_sem=cell_rs.at[r],
                device_id=device(r, 0),
                device_id_type=MESH,
            ),
            pltpu.make_async_remote_copy(
                src_ref=sens_out.at[peer],
                dst_ref=sens_in.at[r],
                send_sem=sens_ss.at[r],
                recv_sem=sens_rs.at[r],
                device_id=device(r, 0),
                device_id_type=MESH,
            ),
        )

    for r in range(1, nt):
        for copy in trade_copies(r):
            copy.start()
    sens_in[0] = sens_out[me]

    sibling = pltpu.make_async_remote_copy(
        src_ref=st_out.at[core],
        dst_ref=st_out.at[core],
        send_sem=sib_ss,
        recv_sem=sib_rs,
        device_id=device(0, 1),
        device_id_type=MESH,
    )
    sibling.start()

    loads[5].wait()
    chi[...] = jnp.zeros_like(chi)
    clo[...] = jnp.zeros_like(clo)
    corr = corr_ref[...]
    top = corr.astype(BF)
    chi[0:nb, 0:nb] = top
    clo[0:nb, 0:nb] = (corr - top.astype(F32)).astype(BF)

    hi_iota = lax.broadcasted_iota(jnp.int32, (HI, LANES), 0).astype(F32).astype(BF)
    lo_iota = lax.broadcasted_iota(jnp.int32, (LO, LANES), 0).astype(F32).astype(BF)
    lo_lane = lax.broadcasted_iota(jnp.int32, (LANES, LO), 1).astype(F32).astype(BF)
    one, zero = jnp.ones((), BF), jnp.zeros((), BF)

    def spread(ref, row, n):
        x = jnp.broadcast_to(ref[pl.ds(row, 1), :], (16, LANES)).astype(BF)
        return jnp.broadcast_to(x[None], (n // 16, 16, LANES)).reshape(n, LANES)

    def net_block(src):
        base = src * rows
        cells = cell_in[src]
        h = lax.shift_right_logical(cells, 8)
        low = (cells - h * LO).astype(F32)
        hi_f[base : base + rows, :] = h.astype(F32)
        lo_f[base : base + rows, :] = low
        s_f[base : base + rows, :] = sens_in[src].astype(F32)
        column = low.T.astype(BF)
        left, right = [], []
        for i in range(rows):
            left.append(
                jnp.where(
                    spread(hi_f, base + i, HI) == hi_iota, spread(s_f, base + i, HI), zero
                )
            )
            right.append(
                jnp.where(
                    jnp.broadcast_to(column[:, i : i + 1], (LANES, LO)) == lo_lane, one, zero
                )
            )
        return jnp.dot(
            jnp.concatenate(left, axis=1),
            jnp.concatenate(right, axis=0),
            preferred_element_type=F32,
        )

    acc[...] = net_block(0)

    for r in range(1, nt):
        for copy in trade_copies(r):
            copy.wait_recv()

    sibling.wait_recv()

    def state_copy(k):
        return pltpu.make_async_remote_copy(
            src_ref=st_out,
            dst_ref=st_in.at[chip],
            send_sem=st_ss,
            recv_sem=st_rs,
            device_id=along(k),
            device_id_type=MESH,
        )

    def send_state(k, c):
        state_copy(k).start()
        return c

    lax.fori_loop(1, nchip, send_state, 0)
    st_in[chip] = st_out[...]

    total = acc[...]
    for r in range(1, nt):
        total = total + net_block(r)
    acc[...] = total

    loads[6].wait()
    loads[7].wait()
    rw = jnp.concatenate(
        [rw_ref[...].reshape(1, nb), jnp.zeros((1, GROUPS * LO - nb), F32)], axis=1
    )
    weighted = [
        acc[g * SETS : (g + 1) * SETS, :] * rw[:, g * LO : (g + 1) * LO] for g in range(GROUPS)
    ]
    w = jnp.concatenate(weighted, axis=1)
    w_hi = w.astype(BF)
    w_lo = (w - w_hi.astype(F32)).astype(BF)
    cw = (
        jnp.dot(w_hi, chi[...], preferred_element_type=F32)
        + jnp.dot(w_hi, clo[...], preferred_element_type=F32)
        + jnp.dot(w_lo, chi[...], preferred_element_type=F32)
    )
    margin = jnp.sqrt(jnp.sum(w * cw, axis=1, keepdims=True) + 1.0)
    weight = dw_ref[me // per_date]
    net_grad = ((weight * rw) * cw / margin).astype(BF)
    for g in range(GROUPS):
        grad[g * SETS : (g + 1) * SETS, :] = net_grad[:, g * LO : (g + 1) * LO]

    def pick_block(dst, slot):
        base = pl.multiple_of(dst * rows, rows)
        right = jnp.concatenate(
            [
                jnp.where(spread(lo_f, base + i, LO) == lo_iota, one, zero)
                for i in range(rows)
            ],
            axis=1,
        )
        product = jnp.dot(grad[...], right, preferred_element_type=F32).astype(BF)
        for i in range(rows):
            kept = jnp.where(
                spread(hi_f, base + i, HI) == hi_iota,
                product[:, i * LANES : (i + 1) * LANES],
                zero,
            ).reshape(HI // 16, 16, LANES)
            tot = kept[0]
            for j in range(1, HI // 16):
                tot = tot + kept[j]
            tot = tot.astype(F32)
            tgp[slot, i * 8 : (i + 1) * 8, :] = tot[:8] + tot[8:]
        for p in range(2):
            tots = []
            for g in range(half // 8):
                at = (p * half + g * 8) * 8
                tot = tgp[slot, pl.ds(at, 8, stride=8), :]
                for s in range(1, 8):
                    tot = tot + tgp[slot, pl.ds(at + s, 8, stride=8), :]
                tots.append(tot)
            tg[dst, p] = jnp.concatenate(tots, axis=0).astype(BF)

    def pick_copy(r, other):
        return pltpu.make_async_remote_copy(
            src_ref=tg.at[lax.rem(nt - r, nt), core + other * (1 - 2 * core)],
            dst_ref=tg_in.at[core * nt + me],
            send_sem=tg_ss.at[2 * r + other],
            recv_sem=tg_rs.at[2 * r + other],
            device_id=device(r, other),
            device_id_type=MESH,
        )

    def pick_step(k, c):
        r = 2 * k + 1
        pick_block(nt - r, 0)
        pick_block(nt - r - 1, 1)
        pick_copy(r, 0).start()
        pick_copy(r, 1).start()
        pick_copy(lax.rem(r + 1, nt), 1).start()

        @pl.when(k < nt // 2 - 1)
        def _():
            pick_copy(r + 1, 0).start()

        return c

    lax.fori_loop(0, nt // 2, pick_step, 0)
    tg_in[core * nt + me] = tg[0, core]
    for r in range(nt):
        for other in range(2):
            if r or other:
                pick_copy(r, other).wait_recv()

    tgx[...] = tg_in[...].reshape(tgx.shape).astype(F32)
    for c in range(half):
        msg[c] = jnp.concatenate(
            [tgx[pl.ds(p * nt * half + c, nt, stride=half), :] for p in range(2)], axis=0
        ).astype(BF)

    def send_grad(k, c):
        pltpu.make_async_remote_copy(
            src_ref=msg.at[lax.rem(chip + k, nchip)],
            dst_ref=pr.at[chip],
            send_sem=pr_ss,
            recv_sem=pr_rs,
            device_id=along(k),
            device_id_type=MESH,
        ).start()
        return c

    lax.fori_loop(1, nchip, send_grad, 0)
    pr[chip] = msg[chip]

    others = pl.ds(0, nchip - 1)
    pltpu.make_async_copy(st_in.at[others], st_in.at[others], st_rs).wait()
    pairs = npath * nt
    ks = table_ref.shape[1]
    states = st_in[...].reshape(pairs, LANES)
    hot = jnp.where(
        states == lax.broadcasted_iota(jnp.int32, (pairs, LANES), 1).astype(F32), 1.0, 0.0
    ).astype(BF)
    tab = jnp.concatenate(split3(table_ref[...].reshape(DATES * ks, LANES)), axis=0)
    at_date = lax.rem(
        lax.broadcasted_iota(jnp.int32, (3 * DATES * ks, pairs), 0) // ks, DATES
    )
    pair_date = lax.rem(
        lax.broadcasted_iota(jnp.int32, (3 * DATES * ks, pairs), 1), nt
    ) // per_date
    basis = jnp.where(
        at_date == pair_date, lax.dot_general(tab, hot, NT, preferred_element_type=F32), 0.0
    ).astype(BF)

    pltpu.make_async_copy(pr.at[others], pr.at[others], pr_rs).wait()
    total = jnp.dot(basis, pr[...].reshape(pairs, LANES), preferred_element_type=F32)
    total = total.reshape(3, DATES, ks, LANES)
    out_ref[...] = total[0] + total[1] + total[2]

    for r in range(1, nt):
        for copy in trade_copies(r):
            copy.wait_send()
    for r in range(nt):
        for other in range(2):
            if r or other:
                pick_copy(r, other).wait_send()
    sibling.wait_send()
    pltpu.make_async_copy(st_in.at[others], st_in.at[others], st_ss).wait()
    pltpu.make_async_copy(pr.at[others], pr.at[others], pr_ss).wait()


def per_device(coef, set_ids, bucket_ids, states, table, risk_weight, correlation, date_weight):
    nt = lax.axis_size("trade")
    npath = lax.axis_size("path")
    trades = coef.shape[2]
    rows = trades // LANES
    nb = correlation.shape[0]
    ks = table.shape[1]
    vmem = pl.BlockSpec(memory_space=pltpu.VMEM)
    hbm = pl.BlockSpec(memory_space=pltpu.HBM)
    dma = pltpu.SemaphoreType.DMA
    return pl.pallas_call(
        functools.partial(kernel, nt, npath),
        out_shape=jax.ShapeDtypeStruct((DATES, ks, LANES), F32),
        in_specs=[hbm] * 8,
        out_specs=vmem,
        scratch_shapes=[
            pltpu.VMEM(coef.shape, F32),
            pltpu.VMEM((rows, LANES), jnp.int32),
            pltpu.VMEM((rows, LANES), jnp.int32),
            pltpu.SMEM(states.shape[::-1], jnp.int32),
            pltpu.VMEM(table.shape, F32),
            pltpu.VMEM((nb,), F32),
            pltpu.VMEM(correlation.shape, F32),
            pltpu.SMEM(date_weight.shape, F32),
            pltpu.VMEM((rows * 8, LANES), F32),
            pltpu.VMEM((nt, rows, LANES), BF),
            pltpu.VMEM((nt, rows, LANES), BF),
            pltpu.VMEM((nt, rows, LANES), jnp.int32),
            pltpu.VMEM((nt * rows, LANES), F32),
            pltpu.VMEM((nt * rows, LANES), F32),
            pltpu.VMEM((nt * rows, LANES), F32),
            pltpu.VMEM((HI, LO), F32),
            pltpu.VMEM((GROUPS * LO, GROUPS * LO), BF),
            pltpu.VMEM((GROUPS * LO, GROUPS * LO), BF),
            pltpu.VMEM((HI, LO), BF),
            pltpu.VMEM((2, rows * 8, LANES), F32),
            pltpu.VMEM((nt, 2, rows // 2, LANES), BF),
            pltpu.VMEM((2 * nt, rows // 2, LANES), BF),
            pltpu.VMEM((nt * rows, LANES), F32),
            pltpu.VMEM((npath // 2, 2 * nt, LANES), BF),
            pltpu.VMEM((npath // 2, 2 * nt, LANES), BF),
            pltpu.VMEM((2, nt, LANES), F32),
            pltpu.VMEM((npath // 2, 2, nt, LANES), F32),
            dma((8,)),
            dma((nt,)),
            dma((nt,)),
            dma((nt,)),
            dma((nt,)),
            dma((2 * nt,)),
            dma((2 * nt,)),
            dma,
            dma,
            dma,
            dma,
            dma,
            dma,
        ],
        compiler_params=pltpu.CompilerParams(
            collective_id=0, has_side_effects=True, vmem_limit_bytes=62 * 1024 * 1024
        ),
    )(
        coef,
        set_ids.reshape(rows, LANES),
        bucket_ids.reshape(rows, LANES),
        states.T,
        table,
        risk_weight,
        correlation,
        date_weight,
    )


def solution(mesh):
    in_specs = (P(None, None, "trade"), P("trade"), P("trade"), P(None, "path"), P(), P(), P(), P())
    out_specs = P(None, None, ("trade", "path"))
    return jax.shard_map(
        per_device, mesh=mesh, in_specs=in_specs, out_specs=out_specs, check_vma=False
    )
```

time: 44.2 us -> 36.3 us (0.82)
  Pallas kernels: 42.2 us -> 34.7 us
    pallas_call x1, Pallas kernels: 42.2 us -> 34.7 us  [per_device(): pl.pallas_call(functools.partial(kernel, nt, npath), out_shape=jax.ShapeD...]
where the time goes in v3:
time: 36.3 us; the launch traced here: 36.1 us
  Pallas kernels  34.7 us (96%)
  local copies, waits for them, and re-layouts  1.38 us (4%)
    pallas_call x1, Pallas kernels, per_device(): pl.pallas_call(functools.partial(kernel, nt, npath), out_shape=jax.ShapeD...  34.7 us
    unnamed x1, local copies, waits for them, and re-layouts  1.38 us

profile of v3, /device:TPU:1, one launch (start us, length us, event | category | flops | bytes accessed | tf_op | source)
XLA Modules:
  0.0 36.1 jit_solution(7401683783902347548)
XLA Ops:
  0.0 34.7 %shard_map.82 = f32[4,16,128]{2,1,0:T(8,128)} custom-call(f32[4,16,4096]{2,1,0:T(8,128)} %coef_hbm.1, s32[32,128]{1,0:T(8,128)} %bitcast.3, s32[32,128]{1,0:T(8,128)} %bitcast.4, s32[2,4]{1,0:T(2,128)} %bitcast.5, f32[4,16,128]{2,1,0:T(8,128)} %table_hbm.1, f32[600]{0:T(1024)} %rw_hbm.1, f32[600,600]{1,0:T(8,128)} %corr_hbm.1, f32[4]{0:T(128)} %dw_hbm.1), custom_call_target="tpu_custom_call" | custom-call | tf_op jit(solution)/shard_map/pallas_call | solution.py:427
  34.7 1.4 %copy.10 = f32[4,16,128]{2,1,0:T(8,128)} copy(f32[4,16,128]{2,1,0:T(8,128)} %shard_map.82) | data formatting | bytes 65536

commit v4 on v3

--- a/solution.py
+++ b/solution.py
@@ -61,7 +61,6 @@
     tgp,
     tg,
     tg_in,
-    tgx,
     msg,
     pr,
     st_out,
@@ -89,6 +88,8 @@
     half = rows // 2
     nb = corr_ref.shape[0]
     per_date = nt // DATES
+    ring = nchip // 2
+    quarter = ring // 2
 
     def device(r, other):
         path = mp + other * (1 - 2 * core)
@@ -100,16 +101,18 @@
     loads = [
         pltpu.make_async_copy(src, dst, load_sem.at[i])
         for i, (src, dst) in enumerate(
-            (
-                (coef_hbm, coef_ref),
-                (table_hbm, table_ref),
-                (st_hbm, st_ref),
+            [
                 (set_hbm, set_ref),
                 (bkt_hbm, bkt_ref),
+                (st_hbm, st_ref),
+                (table_hbm, table_ref),
+            ]
+            + [(coef_hbm.at[d], coef_ref.at[d]) for d in range(DATES)]
+            + [
                 (corr_hbm, corr_ref),
                 (rw_hbm, rw_ref),
                 (dw_hbm, dw_ref),
-            )
+            ]
         )
     ]
     for load in loads:
@@ -129,43 +132,22 @@
 
     lax.fori_loop(1, nchip, greet, 0)
 
-    loads[3].wait()
-    loads[4].wait()
-    for p in range(2):
-        every = pl.ds(p, half, stride=2)
-        bkt = bkt_ref[every, :]
-        group = (bkt >= LO).astype(jnp.int32) + (bkt >= 2 * LO).astype(jnp.int32)
-        cell_in[0, p * half : (p + 1) * half, :] = (
-            (group * SETS + set_ref[every, :]) * LO + bkt - group * LO
-        )
-
-    for load in loads[:3]:
-        load.wait()
-    lane = lax.broadcasted_iota(jnp.int32, table_ref.shape[1:], 1)
-    for d in range(DATES):
-        for p in range(per_date):
-            q = d * per_date + p
-            state = st_ref[p, d]
-            st_out[core, q : q + 1, :] = jnp.full((1, LANES), state, jnp.int32).astype(F32)
-            col = jnp.sum(
-                jnp.where(lane == state, table_ref[d], 0.0), axis=1, keepdims=True
+    def place(c):
+        y, z, k = c // (2 * ring), c // 2 % ring, c % 2
+        return ((z // quarter * 2 + k) * 2 + y) * quarter + z % quarter
+
+    loads[0].wait()
+    loads[1].wait()
+    for c in range(rows):
+        if c // 2 % quarter == 0:
+            every = pl.ds(c, quarter, stride=2)
+            bkt = bkt_ref[every, :]
+            group = (bkt >= LO).astype(jnp.int32) + (bkt >= 2 * LO).astype(jnp.int32)
+            cell_in[0, place(c) : place(c) + quarter, :] = (
+                (group * SETS + set_ref[every, :]) * LO + bkt - group * LO
             )
-            for c in range(rows):
-                x = coef_ref[d, :, c * LANES : (c + 1) * LANES] * col
-                at = (c % 2) * half + c // 2
-                part[at * 8 : (at + 1) * 8, :] = x[:8] + x[8:]
-            tots = []
-            for g in range(rows // 8):
-                tot = part[pl.ds(g * 64, 8, stride=8), :]
-                for s in range(1, 8):
-                    tot = tot + part[pl.ds(g * 64 + s, 8, stride=8), :]
-                tots.append(tot)
-            sens_out[q] = jnp.concatenate(tots, axis=0).astype(BF)
-
-    pl.semaphore_wait(barrier, 2 * nt - 1 + nchip - 1)
 
     def trade_copies(r):
-        peer = lax.rem(me + r, nt)
         return (
             pltpu.make_async_remote_copy(
                 src_ref=cell_in.at[0],
@@ -176,7 +158,7 @@
                 device_id_type=MESH,
             ),
             pltpu.make_async_remote_copy(
-                src_ref=sens_out.at[peer],
+                src_ref=sens_out.at[r],
                 dst_ref=sens_in.at[r],
                 send_sem=sens_ss.at[r],
                 recv_sem=sens_rs.at[r],
@@ -185,22 +167,64 @@
             ),
         )
 
-    for r in range(1, nt):
-        for copy in trade_copies(r):
-            copy.start()
-    sens_in[0] = sens_out[me]
-
+    pl.semaphore_wait(barrier, 2 * nt - 1 + nchip - 1)
+    far = sorted(range(nt), key=lambda r: -min(r, nt - r))
+    for r in far[:-1]:
+        trade_copies(r)[0].start()
+
+    for load in loads[2 : 4 + DATES]:
+        load.wait()
+    lane = lax.broadcasted_iota(jnp.int32, table_ref.shape[1:], 1)
+    for r in far:
+        q = lax.rem(me + r, nt)
+        d = q // per_date
+        state = st_ref[lax.rem(q, per_date), d]
+        col = jnp.sum(jnp.where(lane == state, table_ref[d], 0.0), axis=1, keepdims=True)
+        for c in range(rows):
+            x = coef_ref[d, :, c * LANES : (c + 1) * LANES] * col
+            at = place(c)
+            part[at * 8 : (at + 1) * 8, :] = x[:8] + x[8:]
+        tots = []
+        for g in range(rows // 8):
+            tot = part[pl.ds(g * 64, 8, stride=8), :]
+            for s in range(1, 8):
+                tot = tot + part[pl.ds(g * 64 + s, 8, stride=8), :]
+            tots.append(tot)
+        if r:
+            sens_out[r] = jnp.concatenate(tots, axis=0).astype(BF)
+            trade_copies(r)[1].start()
+        else:
+            sens_in[0] = jnp.concatenate(tots, axis=0).astype(BF)
+
+    for d in range(DATES):
+        for p in range(per_date):
+            q = d * per_date + p
+            st_out[q : q + 1, :] = jnp.full((1, LANES), st_ref[p, d], jnp.int32).astype(F32)
+
+    def send_state(k, c):
+        pltpu.make_async_remote_copy(
+            src_ref=st_out,
+            dst_ref=st_in.at[core, chip],
+            send_sem=st_ss,
+            recv_sem=st_rs,
+            device_id=along(k),
+            device_id_type=MESH,
+        ).start()
+        return c
+
+    lax.fori_loop(1, nchip, send_state, 0)
+    st_in[core, chip] = st_out[...]
+    others = pl.ds(0, nchip - 1)
     sibling = pltpu.make_async_remote_copy(
-        src_ref=st_out.at[core],
-        dst_ref=st_out.at[core],
+        src_ref=st_in.at[core],
+        dst_ref=st_in.at[core],
         send_sem=sib_ss,
         recv_sem=sib_rs,
         device_id=device(0, 1),
         device_id_type=MESH,
     )
-    sibling.start()
-
-    loads[5].wait()
+
+    loads[4 + DATES].wait()
     chi[...] = jnp.zeros_like(chi)
     clo[...] = jnp.zeros_like(clo)
     corr = corr_ref[...]
@@ -250,32 +274,16 @@
         for copy in trade_copies(r):
             copy.wait_recv()
 
-    sibling.wait_recv()
-
-    def state_copy(k):
-        return pltpu.make_async_remote_copy(
-            src_ref=st_out,
-            dst_ref=st_in.at[chip],
-            send_sem=st_ss,
-            recv_sem=st_rs,
-            device_id=along(k),
-            device_id_type=MESH,
-        )
-
-    def send_state(k, c):
-        state_copy(k).start()
-        return c
-
-    lax.fori_loop(1, nchip, send_state, 0)
-    st_in[chip] = st_out[...]
-
     total = acc[...]
     for r in range(1, nt):
         total = total + net_block(r)
     acc[...] = total
 
-    loads[6].wait()
-    loads[7].wait()
+    pltpu.make_async_copy(st_in.at[core, others], st_in.at[core, others], st_rs).wait()
+    sibling.start()
+
+    loads[5 + DATES].wait()
+    loads[6 + DATES].wait()
     rw = jnp.concatenate(
         [rw_ref[...].reshape(1, nb), jnp.zeros((1, GROUPS * LO - nb), F32)], axis=1
     )
@@ -296,11 +304,13 @@
     for g in range(GROUPS):
         grad[g * SETS : (g + 1) * SETS, :] = net_grad[:, g * LO : (g + 1) * LO]
 
-    def pick_block(dst, slot):
-        base = pl.multiple_of(dst * rows, rows)
+    def pick_blocks(dst, h, slot):
+        def row(i):
+            return pl.multiple_of(dst * rows + h * half, half) + i // half * rows + i % half
+
         right = jnp.concatenate(
             [
-                jnp.where(spread(lo_f, base + i, LO) == lo_iota, one, zero)
+                jnp.where(spread(lo_f, row(i), LO) == lo_iota, one, zero)
                 for i in range(rows)
             ],
             axis=1,
@@ -308,7 +318,7 @@
         product = jnp.dot(grad[...], right, preferred_element_type=F32).astype(BF)
         for i in range(rows):
             kept = jnp.where(
-                spread(hi_f, base + i, HI) == hi_iota,
+                spread(hi_f, row(i), HI) == hi_iota,
                 product[:, i * LANES : (i + 1) * LANES],
                 zero,
             ).reshape(HI // 16, 16, LANES)
@@ -317,72 +327,81 @@
                 tot = tot + kept[j]
             tot = tot.astype(F32)
             tgp[slot, i * 8 : (i + 1) * 8, :] = tot[:8] + tot[8:]
-        for p in range(2):
-            tots = []
-            for g in range(half // 8):
-                at = (p * half + g * 8) * 8
+        for b in range(2):
+            for k in range(2):
+                at = (b * half + k * 8) * 8
                 tot = tgp[slot, pl.ds(at, 8, stride=8), :]
                 for s in range(1, 8):
                     tot = tot + tgp[slot, pl.ds(at + s, 8, stride=8), :]
-                tots.append(tot)
-            tg[dst, p] = jnp.concatenate(tots, axis=0).astype(BF)
-
-    def pick_copy(r, other):
+                tg[dst + b, h, k] = tot
+
+    def pick_copy(r, h, other):
         return pltpu.make_async_remote_copy(
-            src_ref=tg.at[lax.rem(nt - r, nt), core + other * (1 - 2 * core)],
-            dst_ref=tg_in.at[core * nt + me],
-            send_sem=tg_ss.at[2 * r + other],
-            recv_sem=tg_rs.at[2 * r + other],
+            src_ref=tg.at[lax.rem(nt - r, nt), h, core + other * (1 - 2 * core)],
+            dst_ref=tg_in.at[h, pl.ds(pl.multiple_of((core * nt + me) * 8, 8), 8)],
+            send_sem=tg_ss.at[(h * nt + r) * 2 + other],
+            recv_sem=tg_rs.at[(h * nt + r) * 2 + other],
             device_id=device(r, other),
             device_id_type=MESH,
         )
 
-    def pick_step(k, c):
-        r = 2 * k + 1
-        pick_block(nt - r, 0)
-        pick_block(nt - r - 1, 1)
-        pick_copy(r, 0).start()
-        pick_copy(r, 1).start()
-        pick_copy(lax.rem(r + 1, nt), 1).start()
-
-        @pl.when(k < nt // 2 - 1)
+    def pick_step(n, c):
+        h = n // 2
+        first = (1 - lax.rem(n, 2)) * (nt // 2)
+        pick_blocks(first + 2, h, 0)
+        pick_blocks(first, h, 1)
+        for b in range(nt // 2 - 1, 0, -1):
+            for other in range(2):
+                pick_copy(nt - first - b, h, other).start()
+        pick_copy(lax.rem(nt - first, nt), h, 1).start()
+
+        @pl.when(first > 0)
         def _():
-            pick_copy(r + 1, 0).start()
+            pick_copy(lax.rem(nt - first, nt), h, 0).start()
 
         return c
 
-    lax.fori_loop(0, nt // 2, pick_step, 0)
-    tg_in[core * nt + me] = tg[0, core]
-    for r in range(nt):
-        for other in range(2):
-            if r or other:
-                pick_copy(r, other).wait_recv()
-
-    tgx[...] = tg_in[...].reshape(tgx.shape).astype(F32)
-    for c in range(half):
-        msg[c] = jnp.concatenate(
-            [tgx[pl.ds(p * nt * half + c, nt, stride=half), :] for p in range(2)], axis=0
-        ).astype(BF)
-
-    def send_grad(k, c):
-        pltpu.make_async_remote_copy(
-            src_ref=msg.at[lax.rem(chip + k, nchip)],
+    lax.fori_loop(0, 4, pick_step, 0)
+
+    mine = pl.ds(pl.multiple_of((core * nt + me) * 8, 8), 8)
+    for h in range(2):
+        tg_in[h, mine, :] = tg[0, h, core]
+
+    def send_grad(target):
+        return pltpu.make_async_remote_copy(
+            src_ref=msg.at[target],
             dst_ref=pr.at[chip],
             send_sem=pr_ss,
             recv_sem=pr_rs,
-            device_id=along(k),
+            device_id={"path": target * 2 + core},
             device_id_type=MESH,
-        ).start()
-        return c
-
-    lax.fori_loop(1, nchip, send_grad, 0)
+        )
+
+    y, z = chip // ring, lax.rem(chip, ring)
+    for h in range(2):
+        for r in range(nt):
+            for other in range(2):
+                if r or other:
+                    pick_copy(r, h, other).wait_recv()
+        for c in range(half // 2):
+            msg[c // quarter * ring + h * quarter + c % quarter] = jnp.concatenate(
+                [tg_in[h, pl.ds(k * nt * 8 + c, nt, stride=8), :] for k in range(2)], axis=0
+            ).astype(BF)
+        for k in range(half // 2 - 1, 0, -1):
+            to_z = h * quarter + lax.rem(z + k, quarter)
+            send_grad(lax.rem(y + k // quarter, 2) * ring + to_z).start()
+        same = y * ring + h * quarter + lax.rem(z, quarter)
+
+        @pl.when(same != chip)
+        def _():
+            send_grad(same).start()
+
     pr[chip] = msg[chip]
 
-    others = pl.ds(0, nchip - 1)
-    pltpu.make_async_copy(st_in.at[others], st_in.at[others], st_rs).wait()
+    sibling.wait_recv()
     pairs = npath * nt
     ks = table_ref.shape[1]
-    states = st_in[...].reshape(pairs, LANES)
+    states = jnp.concatenate([st_in[k, c] for c in range(nchip) for k in range(2)], axis=0)
     hot = jnp.where(
         states == lax.broadcasted_iota(jnp.int32, (pairs, LANES), 1).astype(F32), 1.0, 0.0
     ).astype(BF)
@@ -408,9 +427,10 @@
     for r in range(nt):
         for other in range(2):
             if r or other:
-                pick_copy(r, other).wait_send()
+                pick_copy(r, 0, other).wait_send()
+                pick_copy(r, 1, other).wait_send()
     sibling.wait_send()
-    pltpu.make_async_copy(st_in.at[others], st_in.at[others], st_ss).wait()
+    pltpu.make_async_copy(st_in.at[core, others], st_in.at[core, others], st_ss).wait()
     pltpu.make_async_copy(pr.at[others], pr.at[others], pr_ss).wait()
 
 
@@ -450,20 +470,19 @@
             pltpu.VMEM((GROUPS * LO, GROUPS * LO), BF),
             pltpu.VMEM((HI, LO), BF),
             pltpu.VMEM((2, rows * 8, LANES), F32),
-            pltpu.VMEM((nt, 2, rows // 2, LANES), BF),
-            pltpu.VMEM((2 * nt, rows // 2, LANES), BF),
-            pltpu.VMEM((nt * rows, LANES), F32),
+            pltpu.VMEM((nt, 2, 2, 8, LANES), F32),
+            pltpu.VMEM((2, 2 * nt * 8, LANES), F32),
             pltpu.VMEM((npath // 2, 2 * nt, LANES), BF),
             pltpu.VMEM((npath // 2, 2 * nt, LANES), BF),
-            pltpu.VMEM((2, nt, LANES), F32),
-            pltpu.VMEM((npath // 2, 2, nt, LANES), F32),
-            dma((8,)),
+            pltpu.VMEM((nt, LANES), F32),
+            pltpu.VMEM((2, npath // 2, nt, LANES), F32),
+            dma((7 + DATES,)),
             dma((nt,)),
             dma((nt,)),
             dma((nt,)),
             dma((nt,)),
-            dma((2 * nt,)),
-            dma((2 * nt,)),
+            dma((4 * nt,)),
+            dma((4 * nt,)),
             dma,
             dma,
             dma,

time: 36.3 us -> 34.6 us (0.953)
  Pallas kernels: 34.7 us -> 33.1 us
    pallas_call x1, Pallas kernels: 34.7 us -> 33.1 us  [per_device(): pl.pallas_call(functools.partial(kernel, nt, npath), out_shape=jax.ShapeD...]
where the time goes in v4:
time: 34.6 us; the launch traced here: 34.5 us
  Pallas kernels  33.1 us (96%)
  local copies, waits for them, and re-layouts  1.38 us (4%)
    pallas_call x1, Pallas kernels, per_device(): pl.pallas_call(functools.partial(kernel, nt, npath), out_shape=jax.ShapeD...  33.1 us
    unnamed x1, local copies, waits for them, and re-layouts  1.38 us

profile of v4, /device:TPU:1, one launch (start us, length us, event | category | flops | bytes accessed | tf_op | source)
XLA Modules:
  0.0 34.5 jit_solution(12109974282843268308)
XLA Ops:
  0.0 33.1 %shard_map.82 = f32[4,16,128]{2,1,0:T(8,128)} custom-call(f32[4,16,4096]{2,1,0:T(8,128)} %coef_hbm.1, s32[32,128]{1,0:T(8,128)} %bitcast.3, s32[32,128]{1,0:T(8,128)} %bitcast.4, s32[2,4]{1,0:T(2,128)} %bitcast.5, f32[4,16,128]{2,1,0:T(8,128)} %table_hbm.1, f32[600]{0:T(1024)} %rw_hbm.1, f32[600,600]{1,0:T(8,128)} %corr_hbm.1, f32[4]{0:T(128)} %dw_hbm.1), custom_call_target="tpu_custom_call" | custom-call | tf_op jit(solution)/shard_map/pallas_call | solution.py:447
  33.1 1.4 %copy.10 = f32[4,16,128]{2,1,0:T(8,128)} copy(f32[4,16,128]{2,1,0:T(8,128)} %shard_map.82) | data formatting | bytes 65536

commit v5 on v4

--- a/solution.py
+++ b/solution.py
@@ -87,6 +87,7 @@
     rows = set_ref.shape[0]
     half = rows // 2
     nb = corr_ref.shape[0]
+    wide = chi.shape[0]
     per_date = nt // DATES
     ring = nchip // 2
     quarter = ring // 2
@@ -167,10 +168,7 @@
             ),
         )
 
-    pl.semaphore_wait(barrier, 2 * nt - 1 + nchip - 1)
     far = sorted(range(nt), key=lambda r: -min(r, nt - r))
-    for r in far[:-1]:
-        trade_copies(r)[0].start()
 
     for load in loads[2 : 4 + DATES]:
         load.wait()
@@ -192,9 +190,13 @@
             tots.append(tot)
         if r:
             sens_out[r] = jnp.concatenate(tots, axis=0).astype(BF)
-            trade_copies(r)[1].start()
         else:
             sens_in[0] = jnp.concatenate(tots, axis=0).astype(BF)
+
+    pl.semaphore_wait(barrier, 2 * nt - 1 + nchip - 1)
+    for r in far[:-1]:
+        for copy in trade_copies(r):
+            copy.start()
 
     for d in range(DATES):
         for p in range(per_date):
@@ -285,24 +287,31 @@
     loads[5 + DATES].wait()
     loads[6 + DATES].wait()
     rw = jnp.concatenate(
-        [rw_ref[...].reshape(1, nb), jnp.zeros((1, GROUPS * LO - nb), F32)], axis=1
-    )
-    weighted = [
-        acc[g * SETS : (g + 1) * SETS, :] * rw[:, g * LO : (g + 1) * LO] for g in range(GROUPS)
-    ]
-    w = jnp.concatenate(weighted, axis=1)
+        [rw_ref[...].reshape(1, nb), jnp.zeros((1, wide - nb), F32)], axis=1
+    )
+    netted = jnp.concatenate(
+        [
+            acc[g * SETS : (g + 1) * SETS, : min(LO, wide - g * LO)]
+            for g in range(GROUPS)
+        ],
+        axis=1,
+    )
+    w = netted * rw
     w_hi = w.astype(BF)
     w_lo = (w - w_hi.astype(F32)).astype(BF)
-    cw = (
-        jnp.dot(w_hi, chi[...], preferred_element_type=F32)
-        + jnp.dot(w_hi, clo[...], preferred_element_type=F32)
-        + jnp.dot(w_lo, chi[...], preferred_element_type=F32)
-    )
+    both = jnp.dot(
+        jnp.concatenate([w_hi, w_lo], axis=0), chi[...], preferred_element_type=F32
+    )
+    cw = both[:SETS] + both[SETS:] + jnp.dot(w_hi, clo[...], preferred_element_type=F32)
     margin = jnp.sqrt(jnp.sum(w * cw, axis=1, keepdims=True) + 1.0)
     weight = dw_ref[me // per_date]
     net_grad = ((weight * rw) * cw / margin).astype(BF)
     for g in range(GROUPS):
-        grad[g * SETS : (g + 1) * SETS, :] = net_grad[:, g * LO : (g + 1) * LO]
+        part_g = net_grad[:, g * LO : min((g + 1) * LO, wide)]
+        grad[g * SETS : (g + 1) * SETS, : part_g.shape[1]] = part_g
+    grad[(GROUPS - 1) * SETS :, wide - (GROUPS - 1) * LO :] = jnp.zeros(
+        (SETS, GROUPS * LO - wide), BF
+    )
 
     def pick_blocks(dst, h, slot):
         def row(i):
@@ -440,13 +449,14 @@
     trades = coef.shape[2]
     rows = trades // LANES
     nb = correlation.shape[0]
+    wide = -(-nb // LANES) * LANES
     ks = table.shape[1]
     vmem = pl.BlockSpec(memory_space=pltpu.VMEM)
     hbm = pl.BlockSpec(memory_space=pltpu.HBM)
     dma = pltpu.SemaphoreType.DMA
     return pl.pallas_call(
         functools.partial(kernel, nt, npath),
-        out_shape=jax.ShapeDtypeStruct((DATES, ks, LANES), F32),
+        out_shape=pltpu.VMEM((DATES, ks, LANES), F32),
         in_specs=[hbm] * 8,
         out_specs=vmem,
         scratch_shapes=[
@@ -466,8 +476,8 @@
             pltpu.VMEM((nt * rows, LANES), F32),
             pltpu.VMEM((nt * rows, LANES), F32),
             pltpu.VMEM((HI, LO), F32),
-            pltpu.VMEM((GROUPS * LO, GROUPS * LO), BF),
-            pltpu.VMEM((GROUPS * LO, GROUPS * LO), BF),
+            pltpu.VMEM((wide, wide), BF),
+            pltpu.VMEM((wide, wide), BF),
             pltpu.VMEM((HI, LO), BF),
             pltpu.VMEM((2, rows * 8, LANES), F32),
             pltpu.VMEM((nt, 2, 2, 8, LANES), F32),
@@ -491,17 +501,22 @@
             dma,
         ],
         compiler_params=pltpu.CompilerParams(
-            collective_id=0, has_side_effects=True, vmem_limit_bytes=62 * 1024 * 1024
+            collective_id=0, has_side_effects=True, vmem_limit_bytes=48 * 1024 * 1024
         ),
     )(
-        coef,
-        set_ids.reshape(rows, LANES),
-        bucket_ids.reshape(rows, LANES),
-        states.T,
-        table,
-        risk_weight,
-        correlation,
-        date_weight,
+        *(
+            pltpu.with_memory_space_constraint(x, pltpu.HBM)
+            for x in (
+                coef,
+                set_ids.reshape(rows, LANES),
+                bucket_ids.reshape(rows, LANES),
+                states.T,
+                table,
+                risk_weight,
+                correlation,
+                date_weight,
+            )
+        )
     )
 
 

time: 34.6 us -> 32.6 us (0.942)
  Pallas kernels: 33.1 us -> 31.9 us
  local copies, waits for them, and re-layouts: 1.38 us -> 0.62 us
    pallas_call x1, Pallas kernels: 33.1 us -> 31.9 us  [per_device(): pl.pallas_call(functools.partial(kernel, nt, npath), out_shape=pltpu.VMEM...]
    unnamed x1, local copies, waits for them, and re-layouts: 1.38 us -> 0.62 us
where the time goes in v5:
time: 32.6 us; the launch traced here: 32.5 us
  Pallas kernels  31.9 us (98%)
  local copies, waits for them, and re-layouts  0.62 us (2%)
    pallas_call x1, Pallas kernels, per_device(): pl.pallas_call(functools.partial(kernel, nt, npath), out_shape=pltpu.VMEM...  31.9 us

profile of v5, /device:TPU:1, one launch (start us, length us, event | category | flops | bytes accessed | tf_op | source)
XLA Modules:
  0.0 32.5 jit_solution(4989154468704518995)
XLA Ops:
  0.0 31.9 %shard_map.82 = f32[4,16,128]{2,1,0:T(8,128)S(1)} custom-call(f32[4,16,4096]{2,1,0:T(8,128)} %coef_hbm.1, s32[32,128]{1,0:T(8,128)} %bitcast.3, s32[32,128]{1,0:T(8,128)} %bitcast.4, s32[2,4]{1,0:T(2,128)} %bitcast.5, f32[4,16,128]{2,1,0:T(8,128)} %table_hbm.1, f32[600]{0:T(1024)} %rw_hbm.1, f32[600,600]{1,0:T(8,128)} %corr_hbm.1, f32[4]{0:T(128)} %dw_hbm.1), custom_call_target="tpu_custom_call" | custom-call | tf_op jit(solution)/shard_map/pallas_call | solution.py:457
  31.9 0.6 %copy.10 = f32[4,16,128]{2,1,0:T(8,128)} copy(f32[4,16,128]{2,1,0:T(8,128)S(1)} %shard_map.82) | data formatting | bytes 65536

commit v6 on v5

--- a/solution.py
+++ b/solution.py
@@ -153,16 +153,16 @@
             pltpu.make_async_remote_copy(
                 src_ref=cell_in.at[0],
                 dst_ref=cell_in.at[r],
-                send_sem=cell_ss.at[r],
-                recv_sem=cell_rs.at[r],
+                send_sem=cell_ss,
+                recv_sem=cell_rs,
                 device_id=device(r, 0),
                 device_id_type=MESH,
             ),
             pltpu.make_async_remote_copy(
                 src_ref=sens_out.at[r],
                 dst_ref=sens_in.at[r],
-                send_sem=sens_ss.at[r],
-                recv_sem=sens_rs.at[r],
+                send_sem=sens_ss,
+                recv_sem=sens_rs,
                 device_id=device(r, 0),
                 device_id_type=MESH,
             ),
@@ -272,9 +272,12 @@
 
     acc[...] = net_block(0)
 
-    for r in range(1, nt):
-        for copy in trade_copies(r):
-            copy.wait_recv()
+    def wait_all(ref, sem):
+        pltpu.make_async_copy(ref, ref, sem).wait()
+
+    received = pl.ds(1, nt - 1)
+    wait_all(cell_in.at[received], cell_rs)
+    wait_all(sens_in.at[received], sens_rs)
 
     total = acc[...]
     for r in range(1, nt):
@@ -348,8 +351,8 @@
         return pltpu.make_async_remote_copy(
             src_ref=tg.at[lax.rem(nt - r, nt), h, core + other * (1 - 2 * core)],
             dst_ref=tg_in.at[h, pl.ds(pl.multiple_of((core * nt + me) * 8, 8), 8)],
-            send_sem=tg_ss.at[(h * nt + r) * 2 + other],
-            recv_sem=tg_rs.at[(h * nt + r) * 2 + other],
+            send_sem=tg_ss.at[h],
+            recv_sem=tg_rs.at[h],
             device_id=device(r, other),
             device_id_type=MESH,
         )
@@ -388,10 +391,7 @@
 
     y, z = chip // ring, lax.rem(chip, ring)
     for h in range(2):
-        for r in range(nt):
-            for other in range(2):
-                if r or other:
-                    pick_copy(r, h, other).wait_recv()
+        wait_all(tg_in.at[h, pl.ds(0, (2 * nt - 1) * 8)], tg_rs.at[h])
         for c in range(half // 2):
             msg[c // quarter * ring + h * quarter + c % quarter] = jnp.concatenate(
                 [tg_in[h, pl.ds(k * nt * 8 + c, nt, stride=8), :] for k in range(2)], axis=0
@@ -425,21 +425,17 @@
         at_date == pair_date, lax.dot_general(tab, hot, NT, preferred_element_type=F32), 0.0
     ).astype(BF)
 
+    wait_all(cell_in.at[received], cell_ss)
+    wait_all(sens_in.at[received], sens_ss)
+    wait_all(tg_in.at[0, pl.ds(0, (2 * nt - 1) * 8)], tg_ss.at[0])
+    wait_all(tg_in.at[1, pl.ds(0, (2 * nt - 1) * 8)], tg_ss.at[1])
+    sibling.wait_send()
+    pltpu.make_async_copy(st_in.at[core, others], st_in.at[core, others], st_ss).wait()
     pltpu.make_async_copy(pr.at[others], pr.at[others], pr_rs).wait()
     total = jnp.dot(basis, pr[...].reshape(pairs, LANES), preferred_element_type=F32)
     total = total.reshape(3, DATES, ks, LANES)
     out_ref[...] = total[0] + total[1] + total[2]
 
-    for r in range(1, nt):
-        for copy in trade_copies(r):
-            copy.wait_send()
-    for r in range(nt):
-        for other in range(2):
-            if r or other:
-                pick_copy(r, 0, other).wait_send()
-                pick_copy(r, 1, other).wait_send()
-    sibling.wait_send()
-    pltpu.make_async_copy(st_in.at[core, others], st_in.at[core, others], st_ss).wait()
     pltpu.make_async_copy(pr.at[others], pr.at[others], pr_ss).wait()
 
 
@@ -487,12 +483,12 @@
             pltpu.VMEM((nt, LANES), F32),
             pltpu.VMEM((2, npath // 2, nt, LANES), F32),
             dma((7 + DATES,)),
-            dma((nt,)),
-            dma((nt,)),
-            dma((nt,)),
-            dma((nt,)),
-            dma((4 * nt,)),
-            dma((4 * nt,)),
+            dma,
+            dma,
+            dma,
+            dma,
+            dma((2,)),
+            dma((2,)),
             dma,
             dma,
             dma,

time: 32.6 us -> 31.7 us (0.972)
  Pallas kernels: 31.9 us -> 31 us
    pallas_call x1, Pallas kernels: 31.9 us -> 31 us  [per_device(): pl.pallas_call(functools.partial(kernel, nt, npath), out_shape=pltpu.VMEM...]
where the time goes in v6:
time: 31.7 us; the launch traced here: 31.6 us
  Pallas kernels  31 us (98%)
  local copies, waits for them, and re-layouts  0.62 us (2%)
    pallas_call x1, Pallas kernels, per_device(): pl.pallas_call(functools.partial(kernel, nt, npath), out_shape=pltpu.VMEM...  31 us

profile of v6, /device:TPU:1, one launch (start us, length us, event | category | flops | bytes accessed | tf_op | source)
XLA Modules:
  0.0 31.6 jit_solution(5061775642025093170)
XLA Ops:
  0.0 31.0 %shard_map.82 = f32[4,16,128]{2,1,0:T(8,128)S(1)} custom-call(f32[4,16,4096]{2,1,0:T(8,128)} %coef_hbm.1, s32[32,128]{1,0:T(8,128)} %bitcast.3, s32[32,128]{1,0:T(8,128)} %bitcast.4, s32[2,4]{1,0:T(2,128)} %bitcast.5, f32[4,16,128]{2,1,0:T(8,128)} %table_hbm.1, f32[600]{0:T(1024)} %rw_hbm.1, f32[600,600]{1,0:T(8,128)} %corr_hbm.1, f32[4]{0:T(128)} %dw_hbm.1), custom_call_target="tpu_custom_call" | custom-call | tf_op jit(solution)/shard_map/pallas_call | solution.py:453
  31.0 0.6 %copy.10 = f32[4,16,128]{2,1,0:T(8,128)} copy(f32[4,16,128]{2,1,0:T(8,128)S(1)} %shard_map.82) | data formatting | bytes 65536

commit v7 on v6

--- a/solution.py
+++ b/solution.py
@@ -10,8 +10,6 @@
 DATES = 4
 SETS = 64
 LO = 256
-GROUPS = 3
-HI = GROUPS * SETS
 LANES = 128
 MESH = pl.DeviceIdType.MESH
 BF = jnp.bfloat16
@@ -57,6 +55,7 @@
     acc,
     chi,
     clo,
+    gradf,
     grad,
     tgp,
     tg,
@@ -88,6 +87,9 @@
     half = rows // 2
     nb = corr_ref.shape[0]
     wide = chi.shape[0]
+    hi_rows = grad.shape[0]
+    tiles, per_row = wide // LANES, LO // LANES
+    apart = SETS // per_row
     per_date = nt // DATES
     ring = nchip // 2
     quarter = ring // 2
@@ -142,10 +144,8 @@
     for c in range(rows):
         if c // 2 % quarter == 0:
             every = pl.ds(c, quarter, stride=2)
-            bkt = bkt_ref[every, :]
-            group = (bkt >= LO).astype(jnp.int32) + (bkt >= 2 * LO).astype(jnp.int32)
             cell_in[0, place(c) : place(c) + quarter, :] = (
-                (group * SETS + set_ref[every, :]) * LO + bkt - group * LO
+                set_ref[every, :] * wide + bkt_ref[every, :]
             )
 
     def trade_copies(r):
@@ -159,7 +159,7 @@
                 device_id_type=MESH,
             ),
             pltpu.make_async_remote_copy(
-                src_ref=sens_out.at[r],
+                src_ref=sens_out.at[lax.rem(me + r, nt)],
                 dst_ref=sens_in.at[r],
                 send_sem=sens_ss,
                 recv_sem=sens_rs,
@@ -170,13 +170,14 @@
 
     far = sorted(range(nt), key=lambda r: -min(r, nt - r))
 
-    for load in loads[2 : 4 + DATES]:
-        load.wait()
+    loads[2].wait()
+    loads[3].wait()
     lane = lax.broadcasted_iota(jnp.int32, table_ref.shape[1:], 1)
-    for r in far:
-        q = lax.rem(me + r, nt)
+    for q in range(nt):
         d = q // per_date
-        state = st_ref[lax.rem(q, per_date), d]
+        if q % per_date == 0:
+            loads[4 + d].wait()
+        state = st_ref[q % per_date, d]
         col = jnp.sum(jnp.where(lane == state, table_ref[d], 0.0), axis=1, keepdims=True)
         for c in range(rows):
             x = coef_ref[d, :, c * LANES : (c + 1) * LANES] * col
@@ -188,15 +189,13 @@
             for s in range(1, 8):
                 tot = tot + part[pl.ds(g * 64 + s, 8, stride=8), :]
             tots.append(tot)
-        if r:
-            sens_out[r] = jnp.concatenate(tots, axis=0).astype(BF)
-        else:
-            sens_in[0] = jnp.concatenate(tots, axis=0).astype(BF)
+        sens_out[q] = jnp.concatenate(tots, axis=0).astype(BF)
 
     pl.semaphore_wait(barrier, 2 * nt - 1 + nchip - 1)
     for r in far[:-1]:
         for copy in trade_copies(r):
             copy.start()
+    sens_in[0] = sens_out[me]
 
     for d in range(DATES):
         for p in range(per_date):
@@ -234,7 +233,7 @@
     chi[0:nb, 0:nb] = top
     clo[0:nb, 0:nb] = (corr - top.astype(F32)).astype(BF)
 
-    hi_iota = lax.broadcasted_iota(jnp.int32, (HI, LANES), 0).astype(F32).astype(BF)
+    hi_iota = lax.broadcasted_iota(jnp.int32, (hi_rows, LANES), 0).astype(F32).astype(BF)
     lo_iota = lax.broadcasted_iota(jnp.int32, (LO, LANES), 0).astype(F32).astype(BF)
     lo_lane = lax.broadcasted_iota(jnp.int32, (LANES, LO), 1).astype(F32).astype(BF)
     one, zero = jnp.ones((), BF), jnp.zeros((), BF)
@@ -256,7 +255,7 @@
         for i in range(rows):
             left.append(
                 jnp.where(
-                    spread(hi_f, base + i, HI) == hi_iota, spread(s_f, base + i, HI), zero
+                    spread(hi_f, base + i, hi_rows) == hi_iota, spread(s_f, base + i, hi_rows), zero
                 )
             )
             right.append(
@@ -270,7 +269,11 @@
             preferred_element_type=F32,
         )
 
-    acc[...] = net_block(0)
+    def halves(x):
+        for k in range(per_row):
+            acc[k] = x[:, k * LANES : (k + 1) * LANES]
+
+    halves(net_block(0))
 
     def wait_all(ref, sem):
         pltpu.make_async_copy(ref, ref, sem).wait()
@@ -279,10 +282,10 @@
     wait_all(cell_in.at[received], cell_rs)
     wait_all(sens_in.at[received], sens_rs)
 
-    total = acc[...]
+    total = jnp.concatenate([acc[k] for k in range(per_row)], axis=1)
     for r in range(1, nt):
         total = total + net_block(r)
-    acc[...] = total
+    halves(total)
 
     pltpu.make_async_copy(st_in.at[core, others], st_in.at[core, others], st_rs).wait()
     sibling.start()
@@ -292,12 +295,20 @@
     rw = jnp.concatenate(
         [rw_ref[...].reshape(1, nb), jnp.zeros((1, wide - nb), F32)], axis=1
     )
+    def tile(rest, j):
+        at = rest * tiles + j
+        return at % per_row, pl.ds(at // per_row, apart, stride=tiles)
+
+    def tile_of(ref, rest, j):
+        half_row, every = tile(rest, j)
+        return ref[half_row, every, :]
+
     netted = jnp.concatenate(
         [
-            acc[g * SETS : (g + 1) * SETS, : min(LO, wide - g * LO)]
-            for g in range(GROUPS)
+            jnp.concatenate([tile_of(acc, rest, j) for j in range(tiles)], axis=1)
+            for rest in range(per_row)
         ],
-        axis=1,
+        axis=0,
     )
     w = netted * rw
     w_hi = w.astype(BF)
@@ -308,13 +319,14 @@
     cw = both[:SETS] + both[SETS:] + jnp.dot(w_hi, clo[...], preferred_element_type=F32)
     margin = jnp.sqrt(jnp.sum(w * cw, axis=1, keepdims=True) + 1.0)
     weight = dw_ref[me // per_date]
-    net_grad = ((weight * rw) * cw / margin).astype(BF)
-    for g in range(GROUPS):
-        part_g = net_grad[:, g * LO : min((g + 1) * LO, wide)]
-        grad[g * SETS : (g + 1) * SETS, : part_g.shape[1]] = part_g
-    grad[(GROUPS - 1) * SETS :, wide - (GROUPS - 1) * LO :] = jnp.zeros(
-        (SETS, GROUPS * LO - wide), BF
-    )
+    net_grad = (weight * rw) * cw / margin
+    for rest in range(per_row):
+        for j in range(tiles):
+            half_row, every = tile(rest, j)
+            gradf[half_row, every, :] = net_grad[
+                rest * apart : (rest + 1) * apart, j * LANES : (j + 1) * LANES
+            ]
+    grad[...] = jnp.concatenate([gradf[k] for k in range(per_row)], axis=1).astype(BF)
 
     def pick_blocks(dst, h, slot):
         def row(i):
@@ -330,12 +342,12 @@
         product = jnp.dot(grad[...], right, preferred_element_type=F32).astype(BF)
         for i in range(rows):
             kept = jnp.where(
-                spread(hi_f, row(i), HI) == hi_iota,
+                spread(hi_f, row(i), hi_rows) == hi_iota,
                 product[:, i * LANES : (i + 1) * LANES],
                 zero,
-            ).reshape(HI // 16, 16, LANES)
+            ).reshape(hi_rows // 16, 16, LANES)
             tot = kept[0]
-            for j in range(1, HI // 16):
+            for j in range(1, hi_rows // 16):
                 tot = tot + kept[j]
             tot = tot.astype(F32)
             tgp[slot, i * 8 : (i + 1) * 8, :] = tot[:8] + tot[8:]
@@ -446,6 +458,7 @@
     rows = trades // LANES
     nb = correlation.shape[0]
     wide = -(-nb // LANES) * LANES
+    hi_rows = SETS * wide // LO
     ks = table.shape[1]
     vmem = pl.BlockSpec(memory_space=pltpu.VMEM)
     hbm = pl.BlockSpec(memory_space=pltpu.HBM)
@@ -471,10 +484,11 @@
             pltpu.VMEM((nt * rows, LANES), F32),
             pltpu.VMEM((nt * rows, LANES), F32),
             pltpu.VMEM((nt * rows, LANES), F32),
-            pltpu.VMEM((HI, LO), F32),
+            pltpu.VMEM((LO // LANES, hi_rows, LANES), F32),
             pltpu.VMEM((wide, wide), BF),
             pltpu.VMEM((wide, wide), BF),
-            pltpu.VMEM((HI, LO), BF),
+            pltpu.VMEM((LO // LANES, hi_rows, LANES), F32),
+            pltpu.VMEM((hi_rows, LO), BF),
             pltpu.VMEM((2, rows * 8, LANES), F32),
             pltpu.VMEM((nt, 2, 2, 8, LANES), F32),
             pltpu.VMEM((2, 2 * nt * 8, LANES), F32),

time: 31.7 us -> 31.4 us (level)
  Pallas kernels: 31 us -> 30.6 us
    pallas_call x1, Pallas kernels: 31 us -> 30.6 us  [per_device(): pl.pallas_call(functools.partial(kernel, nt, npath), out_shape=pltpu.VMEM...]
where the time goes in v7:
time: 31.4 us; the launch traced here: 31.2 us
  Pallas kernels  30.6 us (97%)
  local copies, waits for them, and re-layouts  0.62 us (2%)
    pallas_call x1, Pallas kernels, per_device(): pl.pallas_call(functools.partial(kernel, nt, npath), out_shape=pltpu.VMEM...  30.6 us

profile of v7, /device:TPU:1, one launch (start us, length us, event | category | flops | bytes accessed | tf_op | source)
XLA Modules:
  0.0 31.2 jit_solution(15137870530041493273)
XLA Ops:
  0.0 30.6 %shard_map.82 = f32[4,16,128]{2,1,0:T(8,128)S(1)} custom-call(f32[4,16,4096]{2,1,0:T(8,128)} %coef_hbm.1, s32[32,128]{1,0:T(8,128)} %bitcast.3, s32[32,128]{1,0:T(8,128)} %bitcast.4, s32[2,4]{1,0:T(2,128)} %bitcast.5, f32[4,16,128]{2,1,0:T(8,128)} %table_hbm.1, f32[600]{0:T(1024)} %rw_hbm.1, f32[600,600]{1,0:T(8,128)} %corr_hbm.1, f32[4]{0:T(128)} %dw_hbm.1), custom_call_target="tpu_custom_call" | custom-call | tf_op jit(solution)/shard_map/pallas_call | solution.py:466
  30.6 0.6 %copy.10 = f32[4,16,128]{2,1,0:T(8,128)} copy(f32[4,16,128]{2,1,0:T(8,128)S(1)} %shard_map.82) | data formatting | bytes 65536

commit v8 on v7

--- a/solution.py
+++ b/solution.py
@@ -54,6 +54,7 @@
     s_f,
     acc,
     chi,
+    cmid,
     clo,
     gradf,
     grad,
@@ -226,12 +227,12 @@
     )
 
     loads[4 + DATES].wait()
-    chi[...] = jnp.zeros_like(chi)
-    clo[...] = jnp.zeros_like(clo)
-    corr = corr_ref[...]
-    top = corr.astype(BF)
-    chi[0:nb, 0:nb] = top
-    clo[0:nb, 0:nb] = (corr - top.astype(F32)).astype(BF)
+    terms = (chi, cmid, clo)
+    for ref, term in zip(terms, split3(corr_ref[...])):
+        below, beside = nb // 16 * 16, nb // LANES * LANES
+        ref[below:, :] = jnp.zeros((wide - below, wide), BF)
+        ref[:, beside:] = jnp.zeros((wide, wide - beside), BF)
+        ref[0:nb, 0:nb] = term
 
     hi_iota = lax.broadcasted_iota(jnp.int32, (hi_rows, LANES), 0).astype(F32).astype(BF)
     lo_iota = lax.broadcasted_iota(jnp.int32, (LO, LANES), 0).astype(F32).astype(BF)
@@ -311,12 +312,14 @@
         axis=0,
     )
     w = netted * rw
-    w_hi = w.astype(BF)
-    w_lo = (w - w_hi.astype(F32)).astype(BF)
-    both = jnp.dot(
-        jnp.concatenate([w_hi, w_lo], axis=0), chi[...], preferred_element_type=F32
-    )
-    cw = both[:SETS] + both[SETS:] + jnp.dot(w_hi, clo[...], preferred_element_type=F32)
+    ws = split3(w)
+    cw = jnp.zeros_like(w)
+    for n in range(1, 4):
+        stacked = jnp.dot(
+            jnp.concatenate(ws[:n], axis=0), terms[3 - n][...], preferred_element_type=F32
+        )
+        for i in range(n - 1, -1, -1):
+            cw = cw + stacked[i * SETS : (i + 1) * SETS]
     margin = jnp.sqrt(jnp.sum(w * cw, axis=1, keepdims=True) + 1.0)
     weight = dw_ref[me // per_date]
     net_grad = (weight * rw) * cw / margin
@@ -487,6 +490,7 @@
             pltpu.VMEM((LO // LANES, hi_rows, LANES), F32),
             pltpu.VMEM((wide, wide), BF),
             pltpu.VMEM((wide, wide), BF),
+            pltpu.VMEM((wide, wide), BF),
             pltpu.VMEM((LO // LANES, hi_rows, LANES), F32),
             pltpu.VMEM((hi_rows, LO), BF),
             pltpu.VMEM((2, rows * 8, LANES), F32),

time: 31.4 us -> 32 us (1.019)
  Pallas kernels: 30.6 us -> 31.2 us
    pallas_call x1, Pallas kernels: 30.6 us -> 31.2 us  [per_device(): pl.pallas_call(functools.partial(kernel, nt, npath), out_shape=pltpu.VMEM...]
where the time goes in v8:
time: 32 us; the launch traced here: 31.8 us
  Pallas kernels  31.2 us (98%)
  local copies, waits for them, and re-layouts  0.62 us (2%)
    pallas_call x1, Pallas kernels, per_device(): pl.pallas_call(functools.partial(kernel, nt, npath), out_shape=pltpu.VMEM...  31.2 us

profile of v8, /device:TPU:1, one launch (start us, length us, event | category | flops | bytes accessed | tf_op | source)
XLA Modules:
  0.0 31.8 jit_solution(16426812045602159752)
XLA Ops:
  0.0 31.2 %shard_map.82 = f32[4,16,128]{2,1,0:T(8,128)S(1)} custom-call(f32[4,16,4096]{2,1,0:T(8,128)} %coef_hbm.1, s32[32,128]{1,0:T(8,128)} %bitcast.3, s32[32,128]{1,0:T(8,128)} %bitcast.4, s32[2,4]{1,0:T(2,128)} %bitcast.5, f32[4,16,128]{2,1,0:T(8,128)} %table_hbm.1, f32[600]{0:T(1024)} %rw_hbm.1, f32[600,600]{1,0:T(8,128)} %corr_hbm.1, f32[4]{0:T(128)} %dw_hbm.1), custom_call_target="tpu_custom_call" | custom-call | tf_op jit(solution)/shard_map/pallas_call | solution.py:469
  31.2 0.6 %copy.10 = f32[4,16,128]{2,1,0:T(8,128)} copy(f32[4,16,128]{2,1,0:T(8,128)S(1)} %shard_map.82) | data formatting | bytes 65536

commit v9 on v8

--- a/solution.py
+++ b/solution.py
@@ -193,9 +193,9 @@
         sens_out[q] = jnp.concatenate(tots, axis=0).astype(BF)
 
     pl.semaphore_wait(barrier, 2 * nt - 1 + nchip - 1)
-    for r in far[:-1]:
-        for copy in trade_copies(r):
-            copy.start()
+    for i in range(2):
+        for r in far[:-1]:
+            trade_copies(r)[i].start()
     sens_in[0] = sens_out[me]
 
     for d in range(DATES):
@@ -243,15 +243,18 @@
         x = jnp.broadcast_to(ref[pl.ds(row, 1), :], (16, LANES)).astype(BF)
         return jnp.broadcast_to(x[None], (n // 16, 16, LANES)).reshape(n, LANES)
 
-    def net_block(src):
+    def unpack(src):
         base = src * rows
         cells = cell_in[src]
         h = lax.shift_right_logical(cells, 8)
         low = (cells - h * LO).astype(F32)
         hi_f[base : base + rows, :] = h.astype(F32)
         lo_f[base : base + rows, :] = low
+        return low.T.astype(BF)
+
+    def net_block(src, column):
+        base = src * rows
         s_f[base : base + rows, :] = sens_in[src].astype(F32)
-        column = low.T.astype(BF)
         left, right = [], []
         for i in range(rows):
             left.append(
@@ -274,18 +277,19 @@
         for k in range(per_row):
             acc[k] = x[:, k * LANES : (k + 1) * LANES]
 
-    halves(net_block(0))
+    halves(net_block(0, unpack(0)))
 
     def wait_all(ref, sem):
         pltpu.make_async_copy(ref, ref, sem).wait()
 
     received = pl.ds(1, nt - 1)
     wait_all(cell_in.at[received], cell_rs)
+    columns = [None] + [unpack(r) for r in range(1, nt)]
     wait_all(sens_in.at[received], sens_rs)
 
     total = jnp.concatenate([acc[k] for k in range(per_row)], axis=1)
     for r in range(1, nt):
-        total = total + net_block(r)
+        total = total + net_block(r, columns[r])
     halves(total)
 
     pltpu.make_async_copy(st_in.at[core, others], st_in.at[core, others], st_rs).wait()

time: 32 us -> 31.7 us (level)
  no operation moved by 1% of the time
where the time goes in v9:
time: 31.7 us; the launch traced here: 31.6 us
  Pallas kernels  30.9 us (97%)
  local copies, waits for them, and re-layouts  0.62 us (2%)
    pallas_call x1, Pallas kernels, per_device(): pl.pallas_call(functools.partial(kernel, nt, npath), out_shape=pltpu.VMEM...  30.9 us

profile of v9, /device:TPU:1, one launch (start us, length us, event | category | flops | bytes accessed | tf_op | source)
XLA Modules:
  0.0 31.6 jit_solution(6761489971813253837)
XLA Ops:
  0.0 30.9 %shard_map.82 = f32[4,16,128]{2,1,0:T(8,128)S(1)} custom-call(f32[4,16,4096]{2,1,0:T(8,128)} %coef_hbm.1, s32[32,128]{1,0:T(8,128)} %bitcast.3, s32[32,128]{1,0:T(8,128)} %bitcast.4, s32[2,4]{1,0:T(2,128)} %bitcast.5, f32[4,16,128]{2,1,0:T(8,128)} %table_hbm.1, f32[600]{0:T(1024)} %rw_hbm.1, f32[600,600]{1,0:T(8,128)} %corr_hbm.1, f32[4]{0:T(128)} %dw_hbm.1), custom_call_target="tpu_custom_call" | custom-call | tf_op jit(solution)/shard_map/pallas_call | solution.py:473
  30.9 0.6 %copy.10 = f32[4,16,128]{2,1,0:T(8,128)} copy(f32[4,16,128]{2,1,0:T(8,128)S(1)} %shard_map.82) | data formatting | bytes 65536
